TPU v7x, 128 devices: a whole 4x4x4 slice. The times are simulated.
128 devices in a mesh: row: 16 (over y, z_lo, core), col: 8 (over z_hi, x).
Axes of the slice: x: 4, y: 4, z: 4 (z_hi: 2, z_lo: 2; z = z_hi * 2 + z_lo), core: 2. Of those that a mesh axis runs over, the one named last changes fastest.
Arguments:
- blocks: bfloat16 [49152, 128, 128], P(('row', 'col')), may hold values from -0.109375 to 0.109375
- block_row: int32 [49152], P(('row', 'col')), may hold values from 0 to 127, as said below
- block_col: int32 [49152], P(('row', 'col')), may hold values from 0 to 255
- random_cols: bfloat16 [8, 16, 2048, 256], P('col', 'row'), may hold values from -6 to 6
- leaf_perm: int32 [128, 2048], P(('row', 'col')), may hold values from 0 to 2047, each once within a row
- parent_perm: int32 [64, 256], replicated, may hold values from 0 to 255, each once within a row
Outputs:
- leaf_basis: float32 [262144, 128], P(('row', 'col'))
- parent_basis: float32 [16384, 128], P(('row', 'col'))
Inputs may be any that keep to these rules, and one draw needn't show every extreme that they name: `block_row`: each device's 384 entries name every block row 0 to 127 at least once.
All inputs are finite; a program needn't handle non-finite values.
Results may differ from a plain program's by a relative error of at most 0.027.
Values may be sent and summed in bfloat16 or wider, within the bound.
A program may use at most 192 MiB of HBM per device.

v0:
```python
import jax
import jax.numpy as jnp
from jax import lax
from jax.sharding import PartitionSpec as P

HI = lax.Precision.HIGHEST


def from_partner(value, axis, apart):
    mask = 2**apart
    pairs = [(source, source ^ mask) for source in range(lax.axis_size(axis))]
    return lax.ppermute(value, axis, pairs)


def interp(full, skel):
    gram = jnp.dot(skel, skel.T, precision=HI, preferred_element_type=jnp.float32)
    cross = jnp.dot(full, skel.T, precision=HI, preferred_element_type=jnp.float32)
    factor = jnp.linalg.cholesky(gram)
    first = lax.linalg.triangular_solve(
        factor, cross, left_side=False, lower=True, transpose_a=True
    )
    return lax.linalg.triangular_solve(
        factor, first, left_side=False, lower=True, transpose_a=False
    )


def local(blocks, block_row, block_col, random_cols, leaf_perm, parent_perm):
    n_col = lax.axis_size("col")
    leaf_rows = random_cols.shape[2]
    width = random_cols.shape[3]
    size_blk = blocks.shape[1]
    count = blocks.shape[0]
    own_rand = random_cols.reshape(leaf_rows, width)
    gathered = lax.all_gather(own_rand, "row", axis=0, tiled=True)
    rand_blocks = gathered.reshape(-1, size_blk, width)
    nrows_blk = leaf_rows * n_col // size_blk
    group = 64
    mats = blocks.reshape(count // group, group, size_blk, size_blk)
    rows_g = block_row.reshape(count // group, group)
    cols_g = block_col.reshape(count // group, group)

    def accumulate(total, items):
        mat, rows, cols = items
        picked = rand_blocks[cols]
        prods = jnp.einsum("gij,gjs->gis", mat, picked, preferred_element_type=jnp.float32)
        return (total + jax.ops.segment_sum(prods, rows, num_segments=nrows_blk), None)

    total0 = jnp.zeros((nrows_blk, size_blk, width), jnp.float32)
    partial_value, _ = lax.scan(accumulate, total0, (mats, rows_g, cols_g))
    partial_value = lax.optimization_barrier(partial_value.astype(jnp.bfloat16)).astype(jnp.float32)
    partial_value = partial_value.reshape(nrows_blk * size_blk, width)
    cindex = lax.axis_index("col")
    leaf_samples = lax.psum_scatter(
        partial_value.astype(jnp.bfloat16), "col", scatter_dimension=0, tiled=True
    ).astype(jnp.float32)
    rank = parent_perm.shape[1] // 2
    skel = leaf_samples[leaf_perm[0, :rank]]
    leaf_basis = interp(leaf_samples, skel)
    other = from_partner(skel.astype(jnp.bfloat16), "col", 0).astype(skel.dtype)
    parity = cindex % 2
    lower = jnp.where(parity == 0, skel, other)
    upper = jnp.where(parity == 0, other, skel)
    stacked = jnp.concatenate([lower, upper], axis=0)
    device = lax.axis_index("row") * n_col + cindex
    perm = lax.dynamic_index_in_dim(parent_perm, device // 2, 0, keepdims=False)
    parent_full = interp(stacked, stacked[perm[:rank]])
    parent_basis = lax.dynamic_slice_in_dim(parent_full, parity * rank, rank, 0)
    return (leaf_basis, parent_basis)


def solution(mesh):
    in_specs = (
        P(("row", "col"), None, None),
        P(("row", "col")),
        P(("row", "col")),
        P("col", "row", None, None),
        P(("row", "col"), None),
        P(),
    )
    out_specs = (P(("row", "col"), None), P(("row", "col"), None))
    return jax.shard_map(local, mesh=mesh, in_specs=in_specs, out_specs=out_specs, check_vma=False)
```

profile of v0, /device:TPU:0, one launch (start us, length us, event | category | flops | bytes accessed | tf_op | source)
XLA Modules:
  0.0 514.8 jit_solution(6466004831060135854)
XLA Ops:
  9.5 94.4 %all-gather.3.cloned.1.call-done = bf16[1,1,32768,256]{3,2,1,0:T(8,128)(2,1)} async-done(((bf16[1,1,2048,256]{3,2,1,0:T(8,128)(2,1)}), bf16[1,1,32768,256]{3,2,1,0:T(8,128)(2,1)}) %all-gather.3.cloned.1.call-update) | async-done | bytes 16777232 | tf_op jit(solution)/shard_map/all_gather | solution.py:34
  103.9 7.8 %broadcast.129 = f32[128,128,256]{2,1,0:T(8,128)} broadcast(f32[]{:T(128)} %constant.95.clone.1), dimensions={} | broadcast | bytes 16777220 | tf_op jit(solution)/shard_map/broadcast.9
  111.7 212.7 %while.10 = (s32[]{:T(128)}, f32[128,128,256]{2,1,0:T(8,128)}, s32[6,64]{1,0:T(8,128)S(1)}, bf16[6,64,128,128]{3,2,1,0:T(8,128)(2,1)}, s32[6,64]{1,0:T(8,128)S(1)}, /*index=5*/bf16[256,128,256]{2,1,0:T(8,128)(2,1)}, s32[]{:T(128)}) while((s32[]{:T(128)}, f32[128,128,256]{2,1,0:T(8,128)}, s32[6,64]{1,0:T(8,128)S(1)}, ...), condition=%wide.region_2.3_spmd, body=%wide.region_0.2_spmd.sunk | while | flops 538969280 | bytes 48240480 | solution.py:49
  111.7 8.5 %gather_fusion = bf16[64,128,256]{2,1,0:T(8,128)(2,1)} fusion(bf16[256,128,256]{2,1,0:T(8,128)(2,1)} %get-tuple-element.106, s32[1024]{0:T(1024)S(1)} %pad_clamp_fusion.4), kind=kCustom, calls=%fused_computation.clone.1 | custom fusion | bytes 8388864 | tf_op jit(solution)/shard_map/while/body/eval_jaxpr/gather | solution.py:44
  120.2 7.3 %fusion.46 = f32[64,128,256]{2,1,0:T(8,128)} fusion(bf16[64,128,256]{2,1,0:T(8,128)(2,1)} %gather_fusion, bf16[6,64,128,128]{3,2,1,0:T(8,128)(2,1)} %get-tuple-element.104, s32[]{:T(128)S(6)} %copy.13), kind=kOutput, calls=%fused_computation.5.clone.1 | convolution fusion | flops 536870912 | bytes 14680068 | tf_op jit(solution)/shard_map/while/body/eval_jaxpr/gij,gjs->gis/dot_general | solution.py:45
  127.5 19.6 %scatter_fusion = f32[128,128,256]{2,1,0:T(8,128)} fusion(f32[128,128,256]{2,1,0:T(8,128)} %get-tuple-element.95, s32[64]{0:T(128)S(1)} %fusion.44, f32[64,128,256]{2,1,0:T(8,128)} %fusion.46), kind=kCustom, calls=%fused_computation.4.clone.1 | custom fusion | flops 2097152 | bytes 25166080 | tf_op jit(solution)/shard_map/while/body/eval_jaxpr/scatter-add | solution.py:46
  147.1 8.5 %gather_fusion = bf16[64,128,256]{2,1,0:T(8,128)(2,1)} fusion(bf16[256,128,256]{2,1,0:T(8,128)(2,1)} %get-tuple-element.106, s32[1024]{0:T(1024)S(1)} %pad_clamp_fusion.4), kind=kCustom, calls=%fused_computation.clone.1 | custom fusion | bytes 8388864 | tf_op jit(solution)/shard_map/while/body/eval_jaxpr/gather | solution.py:44
  155.6 7.3 %fusion.46 = f32[64,128,256]{2,1,0:T(8,128)} fusion(bf16[64,128,256]{2,1,0:T(8,128)(2,1)} %gather_fusion, bf16[6,64,128,128]{3,2,1,0:T(8,128)(2,1)} %get-tuple-element.104, s32[]{:T(128)S(6)} %copy.13), kind=kOutput, calls=%fused_computation.5.clone.1 | convolution fusion | flops 536870912 | bytes 14680068 | tf_op jit(solution)/shard_map/while/body/eval_jaxpr/gij,gjs->gis/dot_general | solution.py:45
  162.9 19.8 %scatter_fusion = f32[128,128,256]{2,1,0:T(8,128)} fusion(f32[128,128,256]{2,1,0:T(8,128)} %get-tuple-element.95, s32[64]{0:T(128)S(1)} %fusion.44, f32[64,128,256]{2,1,0:T(8,128)} %fusion.46), kind=kCustom, calls=%fused_computation.4.clone.1 | custom fusion | flops 2097152 | bytes 25166080 | tf_op jit(solution)/shard_map/while/body/eval_jaxpr/scatter-add | solution.py:46
  182.7 8.5 %gather_fusion = bf16[64,128,256]{2,1,0:T(8,128)(2,1)} fusion(bf16[256,128,256]{2,1,0:T(8,128)(2,1)} %get-tuple-element.106, s32[1024]{0:T(1024)S(1)} %pad_clamp_fusion.4), kind=kCustom, calls=%fused_computation.clone.1 | custom fusion | bytes 8388864 | tf_op jit(solution)/shard_map/while/body/eval_jaxpr/gather | solution.py:44
  191.2 7.3 %fusion.46 = f32[64,128,256]{2,1,0:T(8,128)} fusion(bf16[64,128,256]{2,1,0:T(8,128)(2,1)} %gather_fusion, bf16[6,64,128,128]{3,2,1,0:T(8,128)(2,1)} %get-tuple-element.104, s32[]{:T(128)S(6)} %copy.13), kind=kOutput, calls=%fused_computation.5.clone.1 | convolution fusion | flops 536870912 | bytes 14680068 | tf_op jit(solution)/shard_map/while/body/eval_jaxpr/gij,gjs->gis/dot_general | solution.py:45
  198.4 19.6 %scatter_fusion = f32[128,128,256]{2,1,0:T(8,128)} fusion(f32[128,128,256]{2,1,0:T(8,128)} %get-tuple-element.95, s32[64]{0:T(128)S(1)} %fusion.44, f32[64,128,256]{2,1,0:T(8,128)} %fusion.46), kind=kCustom, calls=%fused_computation.4.clone.1 | custom fusion | flops 2097152 | bytes 25166080 | tf_op jit(solution)/shard_map/while/body/eval_jaxpr/scatter-add | solution.py:46
  218.0 8.5 %gather_fusion = bf16[64,128,256]{2,1,0:T(8,128)(2,1)} fusion(bf16[256,128,256]{2,1,0:T(8,128)(2,1)} %get-tuple-element.106, s32[1024]{0:T(1024)S(1)} %pad_clamp_fusion.4), kind=kCustom, calls=%fused_computation.clone.1 | custom fusion | bytes 8388864 | tf_op jit(solution)/shard_map/while/body/eval_jaxpr/gather | solution.py:44
  226.5 7.3 %fusion.46 = f32[64,128,256]{2,1,0:T(8,128)} fusion(bf16[64,128,256]{2,1,0:T(8,128)(2,1)} %gather_fusion, bf16[6,64,128,128]{3,2,1,0:T(8,128)(2,1)} %get-tuple-element.104, s32[]{:T(128)S(6)} %copy.13), kind=kOutput, calls=%fused_computation.5.clone.1 | convolution fusion | flops 536870912 | bytes 14680068 | tf_op jit(solution)/shard_map/while/body/eval_jaxpr/gij,gjs->gis/dot_general | solution.py:45
  233.8 19.7 %scatter_fusion = f32[128,128,256]{2,1,0:T(8,128)} fusion(f32[128,128,256]{2,1,0:T(8,128)} %get-tuple-element.95, s32[64]{0:T(128)S(1)} %fusion.44, f32[64,128,256]{2,1,0:T(8,128)} %fusion.46), kind=kCustom, calls=%fused_computation.4.clone.1 | custom fusion | flops 2097152 | bytes 25166080 | tf_op jit(solution)/shard_map/while/body/eval_jaxpr/scatter-add | solution.py:46
  253.5 8.5 %gather_fusion = bf16[64,128,256]{2,1,0:T(8,128)(2,1)} fusion(bf16[256,128,256]{2,1,0:T(8,128)(2,1)} %get-tuple-element.106, s32[1024]{0:T(1024)S(1)} %pad_clamp_fusion.4), kind=kCustom, calls=%fused_computation.clone.1 | custom fusion | bytes 8388864 | tf_op jit(solution)/shard_map/while/body/eval_jaxpr/gather | solution.py:44
  262.0 7.3 %fusion.46 = f32[64,128,256]{2,1,0:T(8,128)} fusion(bf16[64,128,256]{2,1,0:T(8,128)(2,1)} %gather_fusion, bf16[6,64,128,128]{3,2,1,0:T(8,128)(2,1)} %get-tuple-element.104, s32[]{:T(128)S(6)} %copy.13), kind=kOutput, calls=%fused_computation.5.clone.1 | convolution fusion | flops 536870912 | bytes 14680068 | tf_op jit(solution)/shard_map/while/body/eval_jaxpr/gij,gjs->gis/dot_general | solution.py:45
  269.3 19.6 %scatter_fusion = f32[128,128,256]{2,1,0:T(8,128)} fusion(f32[128,128,256]{2,1,0:T(8,128)} %get-tuple-element.95, s32[64]{0:T(128)S(1)} %fusion.44, f32[64,128,256]{2,1,0:T(8,128)} %fusion.46), kind=kCustom, calls=%fused_computation.4.clone.1 | custom fusion | flops 2097152 | bytes 25166080 | tf_op jit(solution)/shard_map/while/body/eval_jaxpr/scatter-add | solution.py:46
  288.9 8.5 %gather_fusion = bf16[64,128,256]{2,1,0:T(8,128)(2,1)} fusion(bf16[256,128,256]{2,1,0:T(8,128)(2,1)} %get-tuple-element.106, s32[1024]{0:T(1024)S(1)} %pad_clamp_fusion.4), kind=kCustom, calls=%fused_computation.clone.1 | custom fusion | bytes 8388864 | tf_op jit(solution)/shard_map/while/body/eval_jaxpr/gather | solution.py:44
  297.4 7.3 %fusion.46 = f32[64,128,256]{2,1,0:T(8,128)} fusion(bf16[64,128,256]{2,1,0:T(8,128)(2,1)} %gather_fusion, bf16[6,64,128,128]{3,2,1,0:T(8,128)(2,1)} %get-tuple-element.104, s32[]{:T(128)S(6)} %copy.13), kind=kOutput, calls=%fused_computation.5.clone.1 | convolution fusion | flops 536870912 | bytes 14680068 | tf_op jit(solution)/shard_map/while/body/eval_jaxpr/gij,gjs->gis/dot_general | solution.py:45
  304.7 19.7 %scatter_fusion = f32[128,128,256]{2,1,0:T(8,128)} fusion(f32[128,128,256]{2,1,0:T(8,128)} %get-tuple-element.95, s32[64]{0:T(128)S(1)} %fusion.44, f32[64,128,256]{2,1,0:T(8,128)} %fusion.46), kind=kCustom, calls=%fused_computation.4.clone.1 | custom fusion | flops 2097152 | bytes 25166080 | tf_op jit(solution)/shard_map/while/body/eval_jaxpr/scatter-add | solution.py:46
  324.4 9.0 %convert_element_type.17 = bf16[128,128,256]{2,1,0:T(8,128)(2,1)} convert(f32[128,128,256]{2,1,0:T(8,128)} %get-tuple-element.35) | non-fusion elementwise | flops 4194304 | bytes 25165824 | tf_op jit(solution)/shard_map/convert_element_type | solution.py:50
  334.8 114.9 %reduce-scatter.2.cloned.1.call-done = bf16[2048,256]{1,0:T(8,128)(2,1)} async-done(((bf16[16384,256]{1,0:T(8,128)(2,1)}), bf16[2048,256]{1,0:T(8,128)(2,1)}) %reduce-scatter.2.cloned.1.call-update) | async-done | bytes 1048592 | tf_op jit(solution)/shard_map/reduce_scatter | solution.py:53
  449.7 2.1 gather_fusion.1
  452.1 11.7 %cholesky.44 = f32[128,128]{1,0:T(8,128)S(1)} custom-call(f32[128,128]{1,0:T(8,128)S(1)} %fusion.18), custom_call_target="Cholesky" | custom-call | tf_op jit(solution)/shard_map/jit(cholesky)/cholesky | solution.py:18
  465.2 9.8 %custom-call.12 = f32[1,128,128]{1,2,0:T(8,128)S(1)} custom-call(f32[1,128,128]{2,1,0:T(8,128)S(1)} %fusion.7), custom_call_target="InvertDiagBlocksLowerTriangular" | custom-call | tf_op jit(solution)/shard_map/triangular_solve | solution.py:19
  475.0 1.4 convert_element_type.19
  477.7 1.6 fusion.22
  479.3 1.0 fusion.16
  480.3 2.0 fusion.14
  483.9 11.7 %cholesky.55 = f32[128,128]{1,0:T(8,128)S(1)} custom-call(f32[128,128]{1,0:T(8,128)S(1)} %fusion.13), custom_call_target="Cholesky" | custom-call | tf_op jit(solution)/shard_map/jit(cholesky)/cholesky | solution.py:18
  496.9 9.8 %custom-call.13 = f32[1,128,128]{1,2,0:T(8,128)S(1)} custom-call(f32[1,128,128]{2,1,0:T(8,128)S(1)} %fusion.8), custom_call_target="InvertDiagBlocksLowerTriangular" | custom-call | tf_op jit(solution)/shard_map/triangular_solve | solution.py:19
  (51 shorter events, 10.7 us)
Async XLA Ops:
  7.2 96.7 %all-gather.3.cloned.1.call-start = ((), (), s32[]{:S(2)}) async-start(), calls=%async_computation.2 | async-start | bytes 17825792 | tf_op jit(solution)/shard_map/all_gather | solution.py:34
  7.9 441.8 %reduce-scatter.2.cloned.1.call-start = ((), (), s32[]{:S(2)}) async-start(), calls=%async_computation.1 | async-start | bytes 9437184 | tf_op jit(solution)/shard_map/reduce_scatter | solution.py:53
  477.1 5.1 collective-permute-start
Sparse Core Ops, SparseCore 0:
  9.7 94.1 all-gather.2
  333.5 116.1 reduce-scatter.1
where the time goes:
time: 516 us; the launch traced here: 515 us
  waiting for transfers between devices  210 us (41%)
  other arithmetic  176 us (34%)
  local copies, waits for them, and re-layouts  64.8 us (13%)
  matrix products  49.4 us (10%)
  between operations  14.2 us (3%)
    scatter-add x6, other arithmetic, accumulate(): jax.ops.segment_sum(prods, rows, num_segments=nrows_blk)  118 us
    reduce_scatter x1, waiting for transfers between devices, local(): lax.psum_scatter(partial_value.astype(jnp.bfloat16), 'col', scatter_dimen...  115 us
    all_gather x1, waiting for transfers between devices, local(): gathered = lax.all_gather(own_rand, 'row', axis=0, tiled=True)  94.4 us
    gather x6, local copies, waits for them, and re-layouts, accumulate(): picked = rand_blocks[cols]  51 us
    dot_general x6, matrix products, accumulate(): jnp.einsum('gij,gjs->gis', mat, picked, preferred_element_type=jnp.float32)  43.5 us
    another operation x6, other arithmetic, interp(): factor = jnp.linalg.cholesky(gram)  24.8 us
    another operation x4, other arithmetic, interp(): lax.linalg.triangular_solve(factor, cross, left_side=False, lower=True, t...  20.9 us
  transfers between devices with their start and end apart: 3, of which 2 were waited for; matrix products, arithmetic and copies ran while one was open for 1% of the time, Pallas kernels for 0%

commit v1 on v0

v1 whole, which is shorter than its diff:
```python
import functools

import jax
import jax.numpy as jnp
from jax import lax
from jax.experimental import pallas as pl
from jax.experimental.pallas import tpu as pltpu
from jax.sharding import PartitionSpec as P

HI = lax.Precision.HIGHEST
VMEM = pl.BlockSpec(memory_space=pltpu.VMEM)
SMEM = pl.BlockSpec(memory_space=pltpu.SMEM)
F32 = jnp.float32
BF16 = jnp.bfloat16


def schedule(rows, cols, nrows):
    count = rows.shape[0]
    steps = (count + nrows) // 2
    k = jnp.arange(count, dtype=jnp.int32)
    i = jnp.arange(nrows, dtype=jnp.int32)
    q = jnp.arange(steps, dtype=jnp.int32)
    same = (rows[None, :] == rows[:, None]) & (k[None, :] < k[:, None])
    within = jnp.sum(same.astype(jnp.int32), axis=1)
    held = jnp.sum((rows[None, :] == i[:, None]).astype(jnp.int32), axis=1)
    pairs = (held + 1) // 2
    before = jnp.sum(jnp.where(i[None, :] < i[:, None], pairs[None, :], 0), axis=1)
    base = jnp.sum(jnp.where(i[None, :] < rows[:, None], pairs[None, :], 0), axis=1)
    place = 2 * base + within
    t = jnp.arange(2 * steps, dtype=jnp.int32)
    code = (k + 1) * 65536 + cols
    slots = jnp.sum(jnp.where(t[:, None] == place[None, :], code[None, :], 0), axis=1)
    row = jnp.minimum(jnp.sum(((before + pairs)[None, :] <= q[:, None]).astype(jnp.int32), axis=1), nrows - 1)
    first = jnp.sum((before[None, :] == q[:, None]).astype(jnp.int32), axis=1)
    total = jnp.sum(pairs).reshape(1)
    return slots, row * 2 + first, total


UNROLL = 4


def spmm_kernel(slots, steps, total, blocks, rand, out, acc):
    acc[...] = jnp.zeros_like(acc)

    def pair(q):
        mats, rights = [], []
        for s in range(2):
            code = slots[2 * q + s]
            k = jnp.maximum(lax.shift_right_logical(code, 16) - 1, 0)
            col = jnp.bitwise_and(code, 65535)
            mat = blocks[k]
            mats.append(jnp.where(code > 0, mat, jnp.zeros_like(mat)))
            rights.append(rand[col])
        return jnp.dot(
            jnp.concatenate(mats, axis=1),
            jnp.concatenate(rights, axis=0),
            preferred_element_type=F32,
        )

    def body(g, carry):
        prods = [pair(g * UNROLL + u) for u in range(UNROLL)]
        for u in range(UNROLL):
            info = steps[g * UNROLL + u]
            keep = (1 - jnp.bitwise_and(info, 1)).astype(F32)
            value = acc[...] * keep + prods[u]
            acc[...] = value
            out[lax.shift_right_logical(info, 1)] = value.astype(BF16)
        return carry

    lax.fori_loop(0, (total[0] + UNROLL - 1) // UNROLL, body, 0)


def spmm(slots, steps, total, blocks, rand, nrows):
    size, width = blocks.shape[1], rand.shape[2]
    return pl.pallas_call(
        spmm_kernel,
        name="spmm",
        out_shape=jax.ShapeDtypeStruct((nrows, size, width), BF16),
        in_specs=[SMEM, SMEM, SMEM, VMEM, VMEM],
        out_specs=VMEM,
        scratch_shapes=[pltpu.VMEM((size, width), F32)],
        compiler_params=pltpu.CompilerParams(vmem_limit_bytes=48 << 20),
    )(slots, steps, total, blocks, rand)


def pick_kernel(perm, full, out):
    lanes = lax.broadcasted_iota(jnp.int32, (perm.shape[0], full.shape[0]), 1)
    hot = jnp.where(lanes == perm[...], 1.0, 0.0).astype(BF16)
    out[...] = jnp.dot(hot, full[...], preferred_element_type=F32).astype(BF16)


def dot_t(a, b):
    return lax.dot_general(a, b, (((1,), (1,)), ((), ())), preferred_element_type=F32)


def inverses(mats):
    n = mats[0].shape[0]
    lane = lax.broadcasted_iota(jnp.int32, (n, n), 1)
    sub = lax.broadcasted_iota(jnp.int32, (n, n), 0)
    lane1 = lax.broadcasted_iota(jnp.int32, (1, n), 1)
    sub1 = lax.broadcasted_iota(jnp.int32, (n, 1), 0)
    for k in range(n):
        cross = (lane == k) | (sub == k)
        done = []
        for a in mats:
            inv = 1.0 / a[k : k + 1, k : k + 1]
            row = jnp.where(lane1 == k, -inv, a[k : k + 1, :] * inv)
            col = jnp.where(sub1 == k, -1.0, a[:, k : k + 1])
            done.append(jnp.where(cross, 0.0, a) - col * row)
        mats = done
    return [-a for a in mats]


def solve_kernel(perm, full, own, low, high, basis, parent):
    both = jnp.concatenate([low[...], high[...]], axis=0)
    lanes = lax.broadcasted_iota(jnp.int32, (perm.shape[0], both.shape[0]), 1)
    hot = jnp.where(lanes == perm[...], 1.0, 0.0).astype(BF16)
    skel = jnp.dot(hot, both, preferred_element_type=F32).astype(BF16)
    mine = own[...]
    inv_leaf, inv_parent = inverses([dot_t(mine, mine), dot_t(skel, skel)])
    parent[...] = jnp.dot(dot_t(mine, skel), inv_parent, precision=HI, preferred_element_type=F32)
    tile = 512

    def body(i, carry):
        at = pl.ds(pl.multiple_of(i * tile, tile), tile)
        cross = dot_t(full[at, :], mine)
        basis[at, :] = jnp.dot(cross, inv_leaf, precision=HI, preferred_element_type=F32)
        return carry

    lax.fori_loop(0, full.shape[0] // tile, body, 0)


def local(blocks, block_row, block_col, random_cols, leaf_perm, parent_perm):
    n_col = lax.axis_size("col")
    leaf_rows, width = random_cols.shape[2:]
    size = blocks.shape[1]
    nrows = leaf_rows * n_col // size
    rank = parent_perm.shape[1] // 2
    slots, steps, total = schedule(block_row, block_col, nrows)
    gathered = lax.all_gather(random_cols.reshape(leaf_rows, width), "row", axis=0, tiled=True)
    partial_value = spmm(slots, steps, total, blocks, gathered.reshape(-1, size, width), nrows)
    leaf = lax.psum_scatter(
        partial_value.reshape(nrows * size, width), "col", scatter_dimension=0, tiled=True
    )
    skel = pl.pallas_call(
        pick_kernel,
        name="pick",
        out_shape=jax.ShapeDtypeStruct((rank, width), BF16),
        in_specs=[VMEM, VMEM],
        out_specs=VMEM,
        compiler_params=pltpu.CompilerParams(vmem_limit_bytes=32 << 20),
    )(leaf_perm[0, :rank].reshape(rank, 1), leaf)
    cindex = lax.axis_index("col")
    other = lax.ppermute(skel, "col", [(s, s ^ 1) for s in range(n_col)])
    parity = cindex % 2
    low = jnp.where(parity == 0, skel, other)
    high = jnp.where(parity == 0, other, skel)
    device = lax.axis_index("row") * n_col + cindex
    perm = lax.dynamic_index_in_dim(parent_perm, device // 2, 0, keepdims=False)[:rank]
    return pl.pallas_call(
        solve_kernel,
        name="solve",
        out_shape=(
            jax.ShapeDtypeStruct((leaf_rows, rank), F32),
            jax.ShapeDtypeStruct((rank, rank), F32),
        ),
        in_specs=[VMEM] * 5,
        out_specs=(VMEM, VMEM),
        compiler_params=pltpu.CompilerParams(vmem_limit_bytes=32 << 20),
    )(perm.reshape(rank, 1), leaf, skel, low, high)


def solution(mesh):
    in_specs = (
        P(("row", "col"), None, None),
        P(("row", "col")),
        P(("row", "col")),
        P("col", "row", None, None),
        P(("row", "col"), None),
        P(),
    )
    out_specs = (P(("row", "col"), None), P(("row", "col"), None))
    return jax.shard_map(local, mesh=mesh, in_specs=in_specs, out_specs=out_specs, check_vma=False)
```

time: 516 us -> 276 us (0.53)
  other arithmetic: 176 us -> 4.48 us
  local copies, waits for them, and re-layouts: 64.8 us -> 3.35 us
  matrix products: 49.4 us -> 0 us
  Pallas kernels: 0 us -> 42.5 us
    scatter-add x6 -> x0, other arithmetic: 118 us -> none  [accumulate(): jax.ops.segment_sum(prods, rows, num_segments=nrows_blk)]
    gather x9 -> x0, local copies, waits for them, and re-layouts: 54.6 us -> none  [the longest x6 51 us: accumulate(): picked = rand_blocks[cols]]
    dot_general x10 -> x0, matrix products: 46 us -> none  [the longest x6 43.5 us: accumulate(): jnp.einsum('gij,gjs->gis', mat, picked, preferred_element_type=jnp.float32)]
    another operation x10 -> x0, other arithmetic: 45.7 us -> none  [the longest x6 24.8 us: interp(): factor = jnp.linalg.cholesky(gram)]
    pallas_call x0 -> x3, Pallas kernels: none -> 42.5 us  [the longest x1 27.2 us: spmm(): pl.pallas_call(spmm_kernel, name='spmm', out_shape=jax.ShapeDtypeStruct((...]
    convert_element_type x3 -> x0, other arithmetic: 10.4 us -> none  [the longest x1 9.02 us: local(): partial_value.astype(jnp.bfloat16)]
    another operation x1 -> x2, local copies, waits for them, and re-layouts: 7.82 us -> 0.77 us  [local(): leaf_perm[0, :rank].reshape(rank, 1)]
  transfers between devices with their start and end apart: 3 -> 3, of which waited for: 2 -> 3; matrix products, arithmetic and copies ran while one was open for 1% -> 2% of each run, Pallas kernels for 0% -> 0%
where the time goes in v1:
time: 276 us
  waiting for transfers between devices  211 us (76%)
  Pallas kernels  42.5 us (15%)
  between operations  14.1 us (5%)
  other arithmetic  4.48 us (2%)
  local copies, waits for them, and re-layouts  3.35 us (1%)
    reduce_scatter x1, waiting for transfers between devices, local(): lax.psum_scatter(partial_value.reshape(nrows * size, width), 'col', scatt...  115 us
    all_gather x1, waiting for transfers between devices, local(): lax.all_gather(random_cols.reshape(leaf_rows, width), 'row', axis=0, tile...  91.4 us
    pallas_call x1, Pallas kernels, spmm(): pl.pallas_call(spmm_kernel, name='spmm', out_shape=jax.ShapeDtypeStruct((...  27.2 us
    pallas_call x1, Pallas kernels, local(): pl.pallas_call(solve_kernel, name='solve', out_shape=(jax.ShapeDtypeStruc...  15 us
  transfers between devices with their start and end apart: 3, of which 3 were waited for; matrix products, arithmetic and copies ran while one was open for 2% of the time, Pallas kernels for 0%

profile of v1, /device:TPU:0, one launch (start us, length us, event | category | flops | bytes accessed | tf_op | source)
XLA Modules:
  0.0 275.9 jit_solution(5400835509071152420)
XLA Ops:
  7.2 0.0 copy-start
  7.2 0.0 all-gather.3.cloned.1.call-start
  7.2 0.7 all-gather.3.cloned.1.call-update
  7.9 0.0 reduce-scatter.2.cloned.1.call-start
  8.0 0.8 convert_reduce_fusion.1
  8.8 0.7 fusion.1
  9.4 0.1 select_reduce_fusion.2
  9.5 0.2 convert_reduce_fusion.2
  9.7 0.9 select_reduce_fusion.1
  10.6 1.0 convert_reduce_fusion
  11.6 0.7 multiply_add_fusion
  12.3 0.2 select_reduce_fusion.slots
  12.4 91.4 %all-gather.3.cloned.1.call-done = bf16[1,1,32768,256]{3,2,1,0:T(8,128)(2,1)} async-done(((bf16[1,1,2048,256]{3,2,1,0:T(8,128)(2,1)}), bf16[1,1,32768,256]{3,2,1,0:T(8,128)(2,1)}) %all-gather.3.cloned.1.call-update) | async-done | bytes 16777232 | tf_op jit(solution)/shard_map/all_gather | solution.py:140
  103.9 27.2 %spmm.1 = bf16[128,128,256]{2,1,0:T(8,128)(2,1)} custom-call(s32[512]{0:T(512)S(1)} %select_reduce_fusion.slots, s32[256]{0:T(256)S(1)} %multiply_add_fusion.2.steps, s32[1]{0:T(128)} %bitcast.1.total, bf16[384,128,128]{2,1,0:T(8,128)(2,1)} %blocks.1, bf16[256,128,256]{2,1,0:T(8,128)(2,1)} %bitcast.8), custom_call_target="tpu_custom_call" | custom-call | tf_op jit(solution)/shard_map/spmm/pallas_call | solution.py:75
  131.0 0.0 reduce-scatter.2.cloned.1.call-update
  131.1 0.7 slice_bitcast_fusion
  131.8 0.1 copy.10.perm
  131.9 115.0 %reduce-scatter.2.cloned.1.call-done.full = bf16[2048,256]{1,0:T(8,128)(2,1)} async-done(((bf16[16384,256]{1,0:T(8,128)(2,1)}), bf16[2048,256]{1,0:T(8,128)(2,1)}) %reduce-scatter.2.cloned.1.call-update) | async-done | bytes 1048592 | tf_op jit(solution)/shard_map/reduce_scatter | solution.py:142
  246.8 0.0 copy-start.1
  246.8 1.2 copy-done.1
  248.1 0.4 pick.1.own
  248.5 0.4 collective-permute-start
  248.8 0.0 copy-done
  248.8 0.1 copy.11.perm
  249.0 3.8 %collective-permute-done = bf16[128,256]{1,0:T(8,128)(2,1)S(1)} collective-permute-done((bf16[128,256]{1,0:T(8,128)(2,1)S(1)}, bf16[128,256]{1,0:T(8,128)(2,1)S(1)}, u32[]{:S(2)}, u32[]{:S(2)}) %collective-permute-start) | collective-permute-done | bytes 65568 | tf_op jit(solution)/shard_map/ppermute | solution.py:154
  252.8 0.0 copy-start.2
  252.8 1.2 copy-done.2
  254.0 15.0 %solve.1 = (f32[2048,128]{1,0:T(8,128)}, f32[128,128]{1,0:T(8,128)}) custom-call(s32[128,1]{1,0:T(8,128)S(1)} %copy.11.perm, bf16[2048,256]{1,0:T(8,128)(2,1)S(1)} %copy-done.2, bf16[128,256]{1,0:T(8,128)(2,1)S(1)} %pick.1.own, bf16[128,256]{1,0:T(8,128)(2,1)S(1)} %get-tuple-element.5.low, bf16[128,256]{1,0:T(8,128)(2,1)S(1)} %get-tuple-element.4.high), custom_call_target="tpu_custom_call" | custom-call | tf_op jit(solution)/shard_map/solve/pallas_call | solution.py:160
  (4 shorter events, 0.0 us)
Async XLA Ops:
  7.2 241.7 %copy-start = (s32[64,256]{1,0:T(8,128)S(1)}, s32[64,256]{1,0:T(8,128)}, u32[]{:S(2)}) copy-start(s32[64,256]{1,0:T(8,128)} %param.11) | copy-start | bytes 196612
  7.2 96.7 %all-gather.3.cloned.1.call-start = ((), (), s32[]{:S(2)}) async-start(), calls=%async_computation.2 | async-start | bytes 17825792 | tf_op jit(solution)/shard_map/all_gather | solution.py:140
  7.9 238.9 %reduce-scatter.2.cloned.1.call-start = ((), (), s32[]{:S(2)}) async-start(), calls=%async_computation.1 | async-start | bytes 9437184 | tf_op jit(solution)/shard_map/reduce_scatter | solution.py:142
  246.8 1.2 copy-start.1
  248.5 4.3 %collective-permute-start = (bf16[128,256]{1,0:T(8,128)(2,1)S(1)}, bf16[128,256]{1,0:T(8,128)(2,1)S(1)}, u32[]{:S(2)}, u32[]{:S(2)}) collective-permute-start(bf16[128,256]{1,0:T(8,128)(2,1)S(1)} %pick.1.own), channel_id=1, source_target_pairs={{0,1},{1,0},{2,3},{3,2},{4,5},{5,4},{6,7},{7,6},{8,9},{9,8},{10,11... | collective-permute-start | bytes 196616 | tf_op jit(solution)/shard_map/ppermute | solution.py:154
  252.8 1.2 copy-start.2
Sparse Core Ops, SparseCore 0:
  9.7 94.1 all-gather.2
  131.2 115.5 reduce-scatter.1

commit v2 on v1

v2 whole, which is shorter than its diff:
```python
import functools

import jax
import jax.numpy as jnp
from jax import lax
from jax.experimental import pallas as pl
from jax.experimental.pallas import tpu as pltpu
from jax.sharding import PartitionSpec as P

HI = lax.Precision.HIGHEST
VMEM = pl.BlockSpec(memory_space=pltpu.VMEM)
SMEM = pl.BlockSpec(memory_space=pltpu.SMEM)
HBM = pl.BlockSpec(memory_space=pltpu.HBM)
F32 = jnp.float32
BF16 = jnp.bfloat16


def schedule(rows, cols, nrows):
    count = rows.shape[0]
    steps = (count + nrows) // 2
    k = jnp.arange(count, dtype=jnp.int32)
    i = jnp.arange(nrows, dtype=jnp.int32)
    q = jnp.arange(steps, dtype=jnp.int32)
    same = (rows[None, :] == rows[:, None]) & (k[None, :] < k[:, None])
    within = jnp.sum(same.astype(jnp.int32), axis=1)
    held = jnp.sum((rows[None, :] == i[:, None]).astype(jnp.int32), axis=1)
    pairs = (held + 1) // 2
    before = jnp.sum(jnp.where(i[None, :] < i[:, None], pairs[None, :], 0), axis=1)
    base = jnp.sum(jnp.where(i[None, :] < rows[:, None], pairs[None, :], 0), axis=1)
    place = 2 * base + within
    t = jnp.arange(2 * steps, dtype=jnp.int32)
    code = (k + 1) * 65536 + cols
    slots = jnp.sum(jnp.where(t[:, None] == place[None, :], code[None, :], 0), axis=1)
    row = jnp.minimum(jnp.sum(((before + pairs)[None, :] <= q[:, None]).astype(jnp.int32), axis=1), nrows - 1)
    first = jnp.sum((before[None, :] == q[:, None]).astype(jnp.int32), axis=1)
    total = jnp.sum(pairs).reshape(1)
    return slots, row * 2 + first, total


MESH = pl.DeviceIdType.MESH


OFFSETS = ((1, 2), (0, 2), (1, 1), (1, 3), (0, 1), (0, 3), (1, 0))


def col_peers():
    c = lax.axis_index("col")
    zh, x = c // 4, lax.rem(c, 4)
    return [lax.rem(zh + dz, 2) * 4 + lax.rem(x + dx, 4) for dz, dx in OFFSETS]


def gather_kernel(
    own, perm, out, perms, local_sem, send_sem, recv_sem, core_send, core_recv, perm_local, perm_send, perm_recv
):
    r = lax.axis_index("row")
    y, zl, co = r // 4, lax.rem(r // 2, 2), lax.rem(r, 2)
    size = own.shape[0]
    half = size // 2
    low = size * 7 // 16
    mid = low + (size - low) // 2

    def at(dy, dz, dc=0):
        return lax.rem(y + dy + 4, 4) * 4 + lax.rem(zl + dz, 2) * 2 + lax.rem(co + dc, 2)

    up, down, side, core = at(1, 0), at(-1, 0), at(0, 1), at(0, 0, 1)
    barrier = pltpu.get_barrier_semaphore()
    for peer in (up, down, side, core):
        pl.semaphore_signal(barrier, inc=1, device_id={"row": peer}, device_id_type=MESH)
    peers = col_peers()
    for j in peers:
        pl.semaphore_signal(barrier, inc=1, device_id={"col": j}, device_id_type=MESH)
    keep = pltpu.make_async_copy(own, out.at[pl.ds(pl.multiple_of(r * size, size), size)], local_sem)
    keep.start()
    keep_perm = pltpu.make_async_copy(perm, perms.at[lax.axis_index("col")], perm_local)
    keep_perm.start()
    pl.semaphore_wait(barrier, 4 + len(peers))

    def rows(source, first, last):
        return pl.ds(pl.multiple_of(source * size + first, 16), last - first)

    sent = []

    def send(source, first, last, target, slot, mine=False):
        dst = out.at[rows(source, first, last)]
        cp = pltpu.make_async_remote_copy(
            src_ref=own.at[pl.ds(first, last - first)] if mine else dst,
            dst_ref=dst,
            send_sem=send_sem.at[len(sent)],
            recv_sem=recv_sem.at[slot],
            device_id={"row": target},
            device_id_type=MESH,
        )
        cp.start()
        sent.append(cp)

    crossed = []

    def cross(source, first, last, mine=False):
        dst = out.at[rows(source, first, last)]
        cp = pltpu.make_async_remote_copy(
            src_ref=own if mine else dst,
            dst_ref=dst,
            send_sem=core_send.at[len(crossed)],
            recv_sem=core_recv.at[len(crossed)],
            device_id={"row": core},
            device_id_type=MESH,
        )
        cp.start()
        crossed.append(cp)

    def arrived(source, first, last, slot):
        dst = out.at[rows(source, first, last)]
        pltpu.make_async_remote_copy(
            src_ref=dst,
            dst_ref=dst,
            send_sem=send_sem.at[0],
            recv_sem=recv_sem.at[slot],
            device_id={"row": core},
            device_id_type=MESH,
        ).wait_recv()

    send(r, 0, half, up, 0, True)
    send(r, half, size, down, 2, True)
    send(r, low, size, side, 4, True)
    send(r, half, size, up, 1, True)
    send(r, 0, half, down, 3, True)
    send(r, 0, low, side, 5, True)
    cross(r, 0, size, True)
    orders = []
    for i, j in enumerate(peers):
        cp = pltpu.make_async_remote_copy(
            src_ref=perm,
            dst_ref=perms.at[lax.axis_index("col")],
            send_sem=perm_send.at[i],
            recv_sem=perm_recv.at[i],
            device_id={"col": j},
            device_id_type=MESH,
        )
        cp.start()
        orders.append(cp)

    prev, nxt, far = at(-1, 0), at(1, 0), at(2, 0)
    zown, zprev, znext, zfar = at(0, 1), at(-1, 1), at(1, 1), at(2, 1)

    arrived(prev, 0, half, 0)
    send(prev, 0, half, up, 6)
    send(prev, 0, low, side, 10)
    cross(prev, 0, half)
    arrived(nxt, half, size, 2)
    send(nxt, half, size, down, 7)
    cross(nxt, half, size)
    arrived(zown, low, size, 4)
    send(zown, low, size, up, 8)
    send(zown, low, size, down, 9)
    cross(zown, low, size)
    arrived(nxt, 0, half, 3)
    send(nxt, 0, low, side, 11)
    cross(nxt, 0, half)
    arrived(prev, half, size, 1)
    cross(prev, half, size)
    arrived(zown, 0, low, 5)
    cross(zown, 0, low)
    arrived(far, 0, half, 6)
    send(far, 0, low, side, 14)
    cross(far, 0, half)
    arrived(far, half, size, 7)
    cross(far, half, size)
    arrived(zprev, low, size, 8)
    send(zprev, low, mid, up, 12)
    cross(zprev, low, size)
    arrived(znext, low, size, 9)
    send(znext, mid, size, down, 13)
    cross(znext, low, size)
    arrived(zprev, 0, low, 10)
    cross(zprev, 0, low)
    arrived(znext, 0, low, 11)
    cross(znext, 0, low)
    arrived(zfar, low, mid, 12)
    cross(zfar, low, mid)
    arrived(zfar, mid, size, 13)
    cross(zfar, mid, size)
    arrived(zfar, 0, low, 14)
    cross(zfar, 0, low)
    keep.wait()
    keep_perm.wait()
    for cp in orders:
        cp.wait()
    for cp in sent:
        cp.wait_send()
    for cp in crossed:
        cp.wait()


def gather(own, perm):
    size, width = own.shape
    count, n_col = lax.axis_size("row"), lax.axis_size("col")
    return pl.pallas_call(
        gather_kernel,
        name="gather",
        out_shape=(
            jax.ShapeDtypeStruct((count * size, width), own.dtype),
            jax.ShapeDtypeStruct((n_col, *perm.shape), perm.dtype),
        ),
        in_specs=[HBM, HBM],
        out_specs=(HBM, HBM),
        scratch_shapes=[
            pltpu.SemaphoreType.DMA,
            pltpu.SemaphoreType.DMA((16,)),
            pltpu.SemaphoreType.DMA((15,)),
            pltpu.SemaphoreType.DMA((16,)),
            pltpu.SemaphoreType.DMA((16,)),
            pltpu.SemaphoreType.DMA,
            pltpu.SemaphoreType.DMA((n_col - 1,)),
            pltpu.SemaphoreType.DMA((n_col - 1,)),
        ],
        compiler_params=pltpu.CompilerParams(collective_id=0, has_side_effects=True),
    )(own, perm)


UNROLL = 4


def spmm_kernel(slots, steps, total, blocks, rand, out, acc):
    acc[...] = jnp.zeros_like(acc)

    def pair(q):
        mats, rights = [], []
        for s in range(2):
            code = slots[2 * q + s]
            k = jnp.maximum(lax.shift_right_logical(code, 16) - 1, 0)
            col = jnp.bitwise_and(code, 65535)
            mat = blocks[k]
            mats.append(jnp.where(code > 0, mat, jnp.zeros_like(mat)))
            rights.append(rand[col])
        return jnp.dot(
            jnp.concatenate(mats, axis=1),
            jnp.concatenate(rights, axis=0),
            preferred_element_type=F32,
        )

    def body(g, carry):
        prods = [pair(g * UNROLL + u) for u in range(UNROLL)]
        for u in range(UNROLL):
            info = steps[g * UNROLL + u]
            keep = (1 - jnp.bitwise_and(info, 1)).astype(F32)
            value = acc[...] * keep + prods[u]
            acc[...] = value
            out[lax.shift_right_logical(info, 1)] = value.astype(BF16)
        return carry

    lax.fori_loop(0, (total[0] + UNROLL - 1) // UNROLL, body, 0)


def spmm(slots, steps, total, blocks, rand, nrows):
    size, width = blocks.shape[1], rand.shape[2]
    return pl.pallas_call(
        spmm_kernel,
        name="spmm",
        out_shape=jax.ShapeDtypeStruct((nrows, size, width), BF16),
        in_specs=[SMEM, SMEM, SMEM, VMEM, VMEM],
        out_specs=VMEM,
        scratch_shapes=[pltpu.VMEM((size, width), F32)],
        compiler_params=pltpu.CompilerParams(vmem_limit_bytes=48 << 20),
    )(slots, steps, total, blocks, rand)


def dot_t(a, b):
    return lax.dot_general(a, b, (((1,), (1,)), ((), ())), preferred_element_type=F32)


def inverse_small(d):
    r = 1.0 / (d[0][0] * d[1][1] - d[0][1] * d[0][1])
    a00, a01, a11 = d[1][1] * r, -d[0][1] * r, d[0][0] * r
    x = [[a00 * d[0][2 + j] + a01 * d[1][2 + j] for j in range(2)], [a01 * d[0][2 + j] + a11 * d[1][2 + j] for j in range(2)]]
    s00 = d[2][2] - (d[0][2] * x[0][0] + d[1][2] * x[1][0])
    s01 = d[2][3] - (d[0][2] * x[0][1] + d[1][2] * x[1][1])
    s11 = d[3][3] - (d[0][3] * x[0][1] + d[1][3] * x[1][1])
    q = 1.0 / (s00 * s11 - s01 * s01)
    c00, c01, c11 = s11 * q, -s01 * q, s00 * q
    y = [[x[i][0] * c00 + x[i][1] * c01, x[i][0] * c01 + x[i][1] * c11] for i in range(2)]
    t00 = a00 + y[0][0] * x[0][0] + y[0][1] * x[0][1]
    t01 = a01 + y[0][0] * x[1][0] + y[0][1] * x[1][1]
    t11 = a11 + y[1][0] * x[1][0] + y[1][1] * x[1][1]
    return [
        [t00, t01, -y[0][0], -y[0][1]],
        [t01, t11, -y[1][0], -y[1][1]],
        [-y[0][0], -y[1][0], c00, c01],
        [-y[0][1], -y[1][1], c01, c11],
    ]


def inverse(a):
    n = a.shape[0]
    group, block = 8, 4
    lane = lax.broadcasted_iota(jnp.int32, (n, n), 1)
    sub = lax.broadcasted_iota(jnp.int32, (n, n), 0)
    lane1 = lax.broadcasted_iota(jnp.int32, (1, n), 1)

    def sweep(g, a):
        for k in range(0, group, block):
            span = range(block)
            d = [[None] * block for _ in span]
            for i in span:
                for j in range(i, block):
                    d[i][j] = jnp.broadcast_to(a[k + i : k + i + 1, k + j : k + j + 1], (1, n))
            inv = inverse_small(d)
            inside1 = (lane1 >= k) & (lane1 < k + block)
            right = [
                jnp.where(lane1 == k + j, -1.0, jnp.where(inside1, 0.0, a[k + j : k + j + 1, :])) for j in span
            ]
            insub = (sub >= k) & (sub < k + block)
            new = jnp.where(insub | ((lane >= k) & (lane < k + block)), 0.0, a)
            for i in span:
                row = inv[i][0] * right[0]
                for j in range(1, block):
                    row = row + inv[i][j] * right[j]
                col = jnp.broadcast_to(a[:, k + i : k + i + 1], (n, n))
                col = jnp.where(sub == k + i, -1.0, jnp.where(insub, 0.0, col))
                new = new - col * row
            a = new
        a = jnp.concatenate([a[group:], a[:group]], axis=0)
        return pltpu.roll(a, n - group, 1)

    return -lax.fori_loop(0, n // group, sweep, a)


def finish_kernel(
    perms, qperm, partial, basis, parent,
    mine, hold, ksend, kin, sibling, wown, win, bout, bin_,
    load_sem, k_s, k_r, s_s, s_r, w_s, w_r, b_s, b_r,
):
    c = lax.axis_index("col")
    leaf = hold.shape[1]
    peers = col_peers()
    n = len(peers)

    def load(i, j):
        return pltpu.make_async_copy(
            partial.at[pl.ds(pl.multiple_of(j * leaf, leaf), leaf)], hold.at[i], load_sem.at[i]
        )

    order = peers + [c]
    for i, j in enumerate(order):
        load(i, j).start()
    barrier = pltpu.get_barrier_semaphore()
    for j in peers:
        pl.semaphore_signal(barrier, inc=1, device_id={"col": j}, device_id_type=MESH)

    def copy(src, dst, send_sem, recv_sem, j):
        return pltpu.make_async_remote_copy(
            src_ref=src, dst_ref=dst, send_sem=send_sem, recv_sem=recv_sem,
            device_id={"col": j}, device_id_type=MESH,
        )

    rank, width = mine.shape
    lanes = lax.broadcasted_iota(jnp.int32, (rank, leaf), 1)

    def pick(i, j):
        hot = jnp.where(lanes == perms[j], 1.0, 0.0).astype(BF16)
        return jnp.dot(hot, hold[i], preferred_element_type=F32)

    kc = []
    for i, j in enumerate(peers):
        load(i, j).wait()
        ksend[i] = pick(i, j).astype(BF16)
        if i == 0:
            pl.semaphore_wait(barrier, n)
        cp = copy(ksend.at[i], kin.at[i], k_s.at[i], k_r.at[i], j)
        cp.start()
        kc.append(cp)
    load(n, c).wait()
    total = pick(n, c)
    for cp in kc:
        cp.wait_recv()
    for i in range(n):
        total = total + kin[i].astype(F32)
    mine[...] = total.astype(BF16)
    to_sibling = copy(mine, sibling, s_s, s_r, c + 1 - 2 * lax.rem(c, 2))
    to_sibling.start()

    skel = mine[...]
    wown[...] = jnp.dot(
        inverse(dot_t(skel, skel)), skel.astype(F32), precision=HI, preferred_element_type=F32
    ).astype(BF16)
    wc = []
    for i, j in enumerate(peers):
        cp = copy(wown, win.at[i], w_s.at[i], w_r.at[i], j)
        cp.start()
        wc.append(cp)

    tile = 512

    def own_rows(t, carry):
        at = pl.ds(pl.multiple_of(t * tile, tile), tile)
        basis[at, :] = dot_t(hold[n, at, :], wown[...])
        return carry

    lax.fori_loop(0, leaf // tile, own_rows, 0)

    back = [OFFSETS.index(((2 - dz) % 2, (4 - dx) % 4)) for dz, dx in OFFSETS]
    bc = []
    for i in range(n):
        wc[back[i]].wait_recv()
        cp = copy(bout.at[i], bin_.at[i], b_s.at[i], b_r.at[i], peers[i])

        def rows(t, carry, i=i):
            at = pl.ds(pl.multiple_of(t * tile, tile), tile)
            bout[i, at, :] = dot_t(hold[i, at, :], win[back[i]]).astype(BF16)
            return carry

        lax.fori_loop(0, leaf // tile, rows, 0)
        cp.start()
        bc.append(cp)

    to_sibling.wait()
    odd = lax.rem(c, 2)
    other = sibling[...]
    low = jnp.where(odd == 0, skel, other)
    high = jnp.where(odd == 0, other, skel)
    both = jnp.concatenate([low, high], axis=0)
    lanes2 = lax.broadcasted_iota(jnp.int32, (rank, 2 * rank), 1)
    hot = jnp.where(lanes2 == qperm[...], 1.0, 0.0).astype(BF16)
    chosen = jnp.dot(hot, both, preferred_element_type=F32).astype(BF16)
    parent[...] = jnp.dot(
        dot_t(skel, chosen), inverse(dot_t(chosen, chosen)), precision=HI, preferred_element_type=F32
    )

    for i in range(n):
        bc[i].wait_recv()

    def add(t, carry):
        at = pl.ds(pl.multiple_of(t * tile, tile), tile)
        value = basis[at, :]
        for i in range(n):
            value = value + bin_[i, at, :].astype(F32)
        basis[at, :] = value
        return carry

    lax.fori_loop(0, leaf // tile, add, 0)
    for cp in kc + wc + bc:
        cp.wait_send()


def finish(perms, qperm, partial):
    count, rank = perms.shape
    width = partial.shape[1]
    leaf = partial.shape[0] // count
    n = count - 1
    dma = pltpu.SemaphoreType.DMA
    return pl.pallas_call(
        finish_kernel,
        name="finish",
        out_shape=(
            jax.ShapeDtypeStruct((leaf, rank), F32),
            jax.ShapeDtypeStruct((rank, rank), F32),
        ),
        in_specs=[VMEM, VMEM, HBM],
        out_specs=(VMEM, VMEM),
        scratch_shapes=[
            pltpu.VMEM((rank, width), BF16),
            pltpu.VMEM((count, leaf, width), BF16),
            pltpu.VMEM((n, rank, width), BF16),
            pltpu.VMEM((n, rank, width), BF16),
            pltpu.VMEM((rank, width), BF16),
            pltpu.VMEM((rank, width), BF16),
            pltpu.VMEM((n, rank, width), BF16),
            pltpu.VMEM((n, leaf, rank), BF16),
            pltpu.VMEM((n, leaf, rank), BF16),
            dma((count,)), dma((n,)), dma((n,)), dma, dma,
            dma((n,)), dma((n,)), dma((n,)), dma((n,)),
        ],
        compiler_params=pltpu.CompilerParams(
            collective_id=1, has_side_effects=True, vmem_limit_bytes=40 << 20
        ),
    )(perms[:, :, None], qperm[:, None], partial)


def local(blocks, block_row, block_col, random_cols, leaf_perm, parent_perm):
    n_col = lax.axis_size("col")
    leaf_rows, width = random_cols.shape[2:]
    size = blocks.shape[1]
    nrows = leaf_rows * n_col // size
    rank = parent_perm.shape[1] // 2
    slots, steps, total = schedule(block_row, block_col, nrows)
    own_perm = jnp.broadcast_to(leaf_perm[:, :rank], (8, rank))
    gathered, perms = gather(random_cols.reshape(leaf_rows, width), own_perm)
    partial_value = spmm(slots, steps, total, blocks, gathered.reshape(-1, size, width), nrows)
    device = lax.axis_index("row") * n_col + lax.axis_index("col")
    qperm = lax.dynamic_index_in_dim(parent_perm, device // 2, 0, keepdims=False)[:rank]
    return finish(perms[:, 0], qperm, partial_value.reshape(nrows * size, width))


def solution(mesh):
    in_specs = (
        P(("row", "col"), None, None),
        P(("row", "col")),
        P(("row", "col")),
        P("col", "row", None, None),
        P(("row", "col"), None),
        P(),
    )
    out_specs = (P(("row", "col"), None), P(("row", "col"), None))
    return jax.shard_map(local, mesh=mesh, in_specs=in_specs, out_specs=out_specs, check_vma=False)
```

time: 276 us -> 192 us (0.70)
  waiting for transfers between devices: 211 us -> 0 us
  Pallas kernels: 42.5 us -> 178 us
  between operations: 14.1 us -> 0.72 us
  local copies, waits for them, and re-layouts: 3.35 us -> 8.15 us
    pallas_call x2, Pallas kernels: 15.4 us -> 151 us  [the longest x1 84.1 us: finish(): pl.pallas_call(finish_kernel, name='finish', out_shape=(jax.ShapeDtypeStr...]
    reduce_scatter x1 -> x0, waiting for transfers between devices: 115 us -> none  [local(): lax.psum_scatter(partial_value.reshape(nrows * size, width), 'col', scatt...]
    all_gather x1 -> x0, waiting for transfers between devices: 91.4 us -> none  [local(): lax.all_gather(random_cols.reshape(leaf_rows, width), 'row', axis=0, tile...]
    ppermute x1 -> x0, waiting for transfers between devices: 3.84 us -> none  [local(): other = lax.ppermute(skel, 'col', [(s, s ^ 1) for s in range(n_col)])]
    unnamed x6, local copies, waits for them, and re-layouts: 2.45 us -> 5.8 us
  transfers between devices with their start and end apart: 3 -> 0, of which waited for: 3 -> 0; matrix products, arithmetic and copies ran while one was open for 2% -> 0% of each run, Pallas kernels for 0% -> 0%
where the time goes in v2:
time: 192 us
  Pallas kernels  178 us (93%)
  local copies, waits for them, and re-layouts  8.15 us (4%)
  other arithmetic  4.46 us (2%)
    pallas_call x1, Pallas kernels, finish(): pl.pallas_call(finish_kernel, name='finish', out_shape=(jax.ShapeDtypeStr...  84.1 us
    pallas_call x1, Pallas kernels, gather(): pl.pallas_call(gather_kernel, name='gather', out_shape=(jax.ShapeDtypeStr...  67.2 us
    pallas_call x1, Pallas kernels, spmm(): pl.pallas_call(spmm_kernel, name='spmm', out_shape=jax.ShapeDtypeStruct((...  26.9 us
    unnamed x6, local copies, waits for them, and re-layouts  5.8 us

profile of v2, /device:TPU:0, one launch (start us, length us, event | category | flops | bytes accessed | tf_op | source)
XLA Modules:
  0.0 191.6 jit_solution(11879047821179531285)
XLA Ops:
  0.6 0.0 copy-start
  0.7 0.8 copy-done
  1.5 0.7 slice_bitcast_fusion
  2.1 0.8 convert_reduce_fusion.1
  2.9 0.7 fusion.1
  3.6 0.1 select_reduce_fusion.2
  3.7 0.2 convert_reduce_fusion.2
  3.9 0.9 select_reduce_fusion.1
  4.8 1.0 convert_reduce_fusion
  5.8 0.7 multiply_add_fusion
  6.5 0.2 select_reduce_fusion.slots
  6.6 0.6 broadcast_in_dim.43.perm
  7.2 0.1 copy.13.qperm
  7.3 67.2 %gather.1 = (bf16[32768,256]{1,0:T(8,128)(2,1)}, s32[8,8,128]{2,1,0:T(8,128)}) custom-call(bf16[2048,256]{1,0:T(8,128)(2,1)} %bitcast.11, s32[8,128]{1,0:T(8,128)} %broadcast_in_dim.43.perm), custom_call_target="tpu_custom_call" | custom-call | tf_op jit(solution)/shard_map/gather/pallas_call | solution.py:197
  74.5 0.8 slice.11
  75.3 26.9 %spmm.1 = bf16[128,128,256]{2,1,0:T(8,128)(2,1)} custom-call(s32[512]{0:T(512)S(1)} %select_reduce_fusion.slots, s32[256]{0:T(256)S(1)} %multiply_add_fusion.2.steps, s32[1]{0:T(128)} %bitcast.4.total, bf16[384,128,128]{2,1,0:T(8,128)(2,1)} %blocks.1, bf16[256,128,256]{2,1,0:T(8,128)(2,1)} %bitcast.10), custom_call_target="tpu_custom_call" | custom-call | tf_op jit(solution)/shard_map/spmm/pallas_call | solution.py:256
  102.2 0.2 copy.12.perms
  102.4 0.0 copy-start.1
  102.4 3.4 %copy-done.1 = bf16[128,128,256]{2,1,0:T(8,128)(2,1)S(1)} copy-done((bf16[128,128,256]{2,1,0:T(8,128)(2,1)S(1)}, bf16[128,128,256]{2,1,0:T(8,128)(2,1)}, u32[]{:S(2)}) %copy-start.1) | copy-done | bytes 8388632
  105.8 84.1 %finish.1 = (f32[2048,128]{1,0:T(8,128)S(1)}, f32[128,128]{1,0:T(8,128)S(1)}) custom-call(s32[8,128,1]{2,1,0:T(8,128)S(1)} %copy.12.perms, s32[128,1]{1,0:T(8,128)S(1)} %copy.13.qperm, bf16[16384,256]{1,0:T(8,128)(2,1)S(1)} %bitcast.9), custom_call_target="tpu_custom_call" | custom-call | tf_op jit(solution)/shard_map/finish/pallas_call | solution.py:450
  190.0 1.0 copy.16
  190.9 0.6 copy.17
  (3 shorter events, 0.0 us)
Async XLA Ops:
  0.6 0.8 copy-start
  102.4 3.4 %copy-start.1 = (bf16[128,128,256]{2,1,0:T(8,128)(2,1)S(1)}, bf16[128,128,256]{2,1,0:T(8,128)(2,1)}, u32[]{:S(2)}) copy-start(bf16[128,128,256]{2,1,0:T(8,128)(2,1)} %spmm.1) | copy-start | bytes 25165828

commit v3 on v2

--- a/solution.py
+++ b/solution.py
@@ -15,26 +15,49 @@
 BF16 = jnp.bfloat16
 
 
-def schedule(rows, cols, nrows):
-    count = rows.shape[0]
-    steps = (count + nrows) // 2
-    k = jnp.arange(count, dtype=jnp.int32)
-    i = jnp.arange(nrows, dtype=jnp.int32)
-    q = jnp.arange(steps, dtype=jnp.int32)
-    same = (rows[None, :] == rows[:, None]) & (k[None, :] < k[:, None])
-    within = jnp.sum(same.astype(jnp.int32), axis=1)
-    held = jnp.sum((rows[None, :] == i[:, None]).astype(jnp.int32), axis=1)
-    pairs = (held + 1) // 2
-    before = jnp.sum(jnp.where(i[None, :] < i[:, None], pairs[None, :], 0), axis=1)
-    base = jnp.sum(jnp.where(i[None, :] < rows[:, None], pairs[None, :], 0), axis=1)
-    place = 2 * base + within
-    t = jnp.arange(2 * steps, dtype=jnp.int32)
-    code = (k + 1) * 65536 + cols
-    slots = jnp.sum(jnp.where(t[:, None] == place[None, :], code[None, :], 0), axis=1)
-    row = jnp.minimum(jnp.sum(((before + pairs)[None, :] <= q[:, None]).astype(jnp.int32), axis=1), nrows - 1)
-    first = jnp.sum((before[None, :] == q[:, None]).astype(jnp.int32), axis=1)
-    total = jnp.sum(pairs).reshape(1)
-    return slots, row * 2 + first, total
+def schedule(rows, cols):
+    count, lanes = rows.shape[1], 128
+    nrows, steps = 128, 256
+
+    def iota(shape, dim):
+        return lax.broadcasted_iota(jnp.int32, shape, dim)
+
+    def ones(mask):
+        return jnp.where(mask, 1, 0)
+
+    def down(value):
+        return jnp.broadcast_to(value, (lanes, count)).T
+
+    rows_k, cols_k = down(rows), down(cols)
+    lane = iota((count, lanes), 1)
+    sub = iota((count, lanes), 0)
+    within = jnp.zeros((count, 1), jnp.int32)
+    for part in range(count // lanes):
+        other = jnp.broadcast_to(rows[:, part * lanes : (part + 1) * lanes], (count, lanes))
+        same = (other == rows_k) & (lane + part * lanes < sub)
+        within = within + jnp.sum(ones(same), axis=1, keepdims=True)
+    held = jnp.sum(ones(rows_k == lane), axis=0, keepdims=True)
+    pairs = lax.shift_right_logical(held + 1, 1)
+    base = jnp.sum(jnp.where(lane < rows_k, jnp.broadcast_to(pairs, (count, lanes)), 0), axis=1, keepdims=True)
+    place = jnp.broadcast_to(2 * base + within, (count, lanes))
+    code = (sub + 1) * 65536 + cols_k
+    lane_r, sub_r = iota((nrows, lanes), 1), iota((nrows, lanes), 0)
+    pairs_all = jnp.broadcast_to(pairs, (nrows, lanes))
+    before = jnp.broadcast_to(
+        jnp.sum(jnp.where(lane_r < sub_r, pairs_all, 0), axis=1, keepdims=True), (nrows, lanes)
+    )
+    end = before + jnp.broadcast_to(
+        jnp.sum(jnp.where(lane_r == sub_r, pairs_all, 0), axis=1, keepdims=True), (nrows, lanes)
+    )
+    out = []
+    for part in range(2 * steps // lanes):
+        out.append(jnp.sum(jnp.where(place == lane + part * lanes, code, 0), axis=0, keepdims=True))
+    for part in range(steps // lanes):
+        q = lane_r + part * lanes
+        row = jnp.minimum(jnp.sum(ones(end <= q), axis=0, keepdims=True), nrows - 1)
+        out.append(2 * row + jnp.sum(ones(before == q), axis=0, keepdims=True))
+    total = jnp.sum(jnp.where(sub_r == 0, jnp.broadcast_to(jnp.max(end, axis=0, keepdims=True), (nrows, lanes)), 0), axis=0, keepdims=True)
+    return out + [total, jnp.zeros_like(total)]
 
 
 MESH = pl.DeviceIdType.MESH
@@ -50,7 +73,8 @@
 
 
 def gather_kernel(
-    own, perm, out, perms, local_sem, send_sem, recv_sem, core_send, core_recv, perm_local, perm_send, perm_recv
+    own, ints, out, perms, plan,
+    perm, local_sem, send_sem, recv_sem, core_send, core_recv, perm_local, perm_send, perm_recv,
 ):
     r = lax.axis_index("row")
     y, zl, co = r // 4, lax.rem(r // 2, 2), lax.rem(r, 2)
@@ -71,6 +95,8 @@
         pl.semaphore_signal(barrier, inc=1, device_id={"col": j}, device_id_type=MESH)
     keep = pltpu.make_async_copy(own, out.at[pl.ds(pl.multiple_of(r * size, size), size)], local_sem)
     keep.start()
+    n_blocks = (ints.shape[1] - perm.shape[1]) // 2
+    perm[...] = jnp.broadcast_to(ints[:, 2 * n_blocks :], perm.shape)
     keep_perm = pltpu.make_async_copy(perm, perms.at[lax.axis_index("col")], perm_local)
     keep_perm.start()
     pl.semaphore_wait(barrier, 4 + len(peers))
@@ -92,6 +118,7 @@
         )
         cp.start()
         sent.append(cp)
+        return cp
 
     crossed = []
 
@@ -138,28 +165,32 @@
         )
         cp.start()
         orders.append(cp)
+    for i, value in enumerate(schedule(ints[:, :n_blocks], ints[:, n_blocks : 2 * n_blocks])):
+        plan[i : i + 1, :] = value
 
     prev, nxt, far = at(-1, 0), at(1, 0), at(2, 0)
     zown, zprev, znext, zfar = at(0, 1), at(-1, 1), at(1, 1), at(2, 1)
 
     arrived(prev, 0, half, 0)
-    send(prev, 0, half, up, 6)
+    far_up = send(prev, 0, half, up, 6)
     send(prev, 0, low, side, 10)
     cross(prev, 0, half)
     arrived(nxt, half, size, 2)
-    send(nxt, half, size, down, 7)
+    far_down = send(nxt, half, size, down, 7)
     cross(nxt, half, size)
-    arrived(zown, low, size, 4)
-    send(zown, low, size, up, 8)
-    send(zown, low, size, down, 9)
-    cross(zown, low, size)
     arrived(nxt, 0, half, 3)
     send(nxt, 0, low, side, 11)
     cross(nxt, 0, half)
     arrived(prev, half, size, 1)
     cross(prev, half, size)
+    arrived(zown, low, size, 4)
+    cross(zown, low, size)
     arrived(zown, 0, low, 5)
     cross(zown, 0, low)
+    far_up.wait_send()
+    send(zown, low, size, up, 8)
+    far_down.wait_send()
+    send(zown, low, size, down, 9)
     arrived(far, 0, half, 6)
     send(far, 0, low, side, 14)
     cross(far, 0, half)
@@ -186,47 +217,52 @@
     for cp in orders:
         cp.wait()
     for cp in sent:
-        cp.wait_send()
+        if cp is not far_up and cp is not far_down:
+            cp.wait_send()
     for cp in crossed:
         cp.wait()
 
 
-def gather(own, perm):
+def gather(own, rows, cols, order):
     size, width = own.shape
     count, n_col = lax.axis_size("row"), lax.axis_size("col")
+    rank = order.shape[0]
+    ints = jnp.concatenate([rows, cols, order])[None, :]
+    dma = pltpu.SemaphoreType.DMA
     return pl.pallas_call(
         gather_kernel,
         name="gather",
         out_shape=(
             jax.ShapeDtypeStruct((count * size, width), own.dtype),
-            jax.ShapeDtypeStruct((n_col, *perm.shape), perm.dtype),
+            jax.ShapeDtypeStruct((n_col, 8, rank), jnp.int32),
+            jax.ShapeDtypeStruct((8, 128), jnp.int32),
         ),
-        in_specs=[HBM, HBM],
-        out_specs=(HBM, HBM),
+        in_specs=[HBM, VMEM],
+        out_specs=(HBM, HBM, VMEM),
         scratch_shapes=[
-            pltpu.SemaphoreType.DMA,
-            pltpu.SemaphoreType.DMA((16,)),
-            pltpu.SemaphoreType.DMA((15,)),
-            pltpu.SemaphoreType.DMA((16,)),
-            pltpu.SemaphoreType.DMA((16,)),
-            pltpu.SemaphoreType.DMA,
-            pltpu.SemaphoreType.DMA((n_col - 1,)),
-            pltpu.SemaphoreType.DMA((n_col - 1,)),
+            pltpu.VMEM((8, rank), jnp.int32),
+            dma, dma((16,)), dma((15,)), dma((16,)), dma((16,)), dma, dma((n_col - 1,)), dma((n_col - 1,)),
         ],
-        compiler_params=pltpu.CompilerParams(collective_id=0, has_side_effects=True),
-    )(own, perm)
+        compiler_params=pltpu.CompilerParams(
+            collective_id=0, has_side_effects=True, vmem_limit_bytes=4 << 20
+        ),
+        cost_estimate=pl.CostEstimate(flops=60000000000, bytes_accessed=40000000, transcendentals=0),
+    )(own, ints)
 
 
 UNROLL = 4
 
 
-def spmm_kernel(slots, steps, total, blocks, rand, out, acc):
+def spmm_kernel(plan, blocks, rand, out, acc):
     acc[...] = jnp.zeros_like(acc)
+    size = acc.shape[0]
+    per = out.shape[1] // size
 
     def pair(q):
         mats, rights = [], []
         for s in range(2):
-            code = slots[2 * q + s]
+            t = 2 * q + s
+            code = plan[t // 128, lax.rem(t, 128)]
             k = jnp.maximum(lax.shift_right_logical(code, 16) - 1, 0)
             col = jnp.bitwise_and(code, 65535)
             mat = blocks[k]
@@ -241,27 +277,30 @@
     def body(g, carry):
         prods = [pair(g * UNROLL + u) for u in range(UNROLL)]
         for u in range(UNROLL):
-            info = steps[g * UNROLL + u]
+            q = g * UNROLL + u
+            info = plan[4 + q // 128, lax.rem(q, 128)]
             keep = (1 - jnp.bitwise_and(info, 1)).astype(F32)
             value = acc[...] * keep + prods[u]
             acc[...] = value
-            out[lax.shift_right_logical(info, 1)] = value.astype(BF16)
+            row = lax.shift_right_logical(info, 1)
+            at = pl.multiple_of(lax.rem(row, per) * size, size)
+            out[row // per, pl.ds(at, size), :] = value.astype(BF16)
         return carry
 
-    lax.fori_loop(0, (total[0] + UNROLL - 1) // UNROLL, body, 0)
-
-
-def spmm(slots, steps, total, blocks, rand, nrows):
+    lax.fori_loop(0, (plan[6, 0] + UNROLL - 1) // UNROLL, body, 0)
+
+
+def spmm(plan, blocks, rand, leaves, leaf_rows):
     size, width = blocks.shape[1], rand.shape[2]
     return pl.pallas_call(
         spmm_kernel,
         name="spmm",
-        out_shape=jax.ShapeDtypeStruct((nrows, size, width), BF16),
-        in_specs=[SMEM, SMEM, SMEM, VMEM, VMEM],
+        out_shape=jax.ShapeDtypeStruct((leaves, leaf_rows, width), BF16),
+        in_specs=[SMEM, VMEM, VMEM],
         out_specs=VMEM,
         scratch_shapes=[pltpu.VMEM((size, width), F32)],
-        compiler_params=pltpu.CompilerParams(vmem_limit_bytes=48 << 20),
-    )(slots, steps, total, blocks, rand)
+        compiler_params=pltpu.CompilerParams(vmem_limit_bytes=4 << 20),
+    )(plan, blocks, rand)
 
 
 def dot_t(a, b):
@@ -325,23 +364,19 @@
 
 
 def finish_kernel(
-    perms, qperm, partial, basis, parent,
-    mine, hold, ksend, kin, sibling, wown, win, bout, bin_,
-    load_sem, k_s, k_r, s_s, s_r, w_s, w_r, b_s, b_r,
+    perms, parent_perm, partial, basis, parent,
+    mine, ksend, kin, sibling, wown, win, zout, zin, xout, xin, yout, yin, vout, vin,
+    k_s, k_r, s_s, s_r, w_s, w_r, z_s, z_r, x_s, x_r, y_s, y_r, v_s, v_r,
 ):
     c = lax.axis_index("col")
-    leaf = hold.shape[1]
+    zh, x = c // 4, lax.rem(c, 4)
+    leaf = partial.shape[1]
     peers = col_peers()
     n = len(peers)
-
-    def load(i, j):
-        return pltpu.make_async_copy(
-            partial.at[pl.ds(pl.multiple_of(j * leaf, leaf), leaf)], hold.at[i], load_sem.at[i]
-        )
-
-    order = peers + [c]
-    for i, j in enumerate(order):
-        load(i, j).start()
+    rank, width = mine.shape
+    cut = zout.shape[1]
+    tile = 256
+
     barrier = pltpu.get_barrier_semaphore()
     for j in peers:
         pl.semaphore_signal(barrier, inc=1, device_id={"col": j}, device_id_type=MESH)
@@ -352,24 +387,24 @@
             device_id={"col": j}, device_id_type=MESH,
         )
 
-    rank, width = mine.shape
     lanes = lax.broadcasted_iota(jnp.int32, (rank, leaf), 1)
 
-    def pick(i, j):
-        hot = jnp.where(lanes == perms[j], 1.0, 0.0).astype(BF16)
-        return jnp.dot(hot, hold[i], preferred_element_type=F32)
+    def down(row):
+        return jnp.broadcast_to(row, (rank, rank)).T[:, :1]
+
+    def pick(j):
+        hot = jnp.where(lanes == down(perms[j, 0:1, :]), 1.0, 0.0).astype(BF16)
+        return jnp.dot(hot, partial[j], preferred_element_type=F32)
 
     kc = []
     for i, j in enumerate(peers):
-        load(i, j).wait()
-        ksend[i] = pick(i, j).astype(BF16)
+        ksend[i] = pick(j).astype(BF16)
         if i == 0:
             pl.semaphore_wait(barrier, n)
         cp = copy(ksend.at[i], kin.at[i], k_s.at[i], k_r.at[i], j)
         cp.start()
         kc.append(cp)
-    load(n, c).wait()
-    total = pick(n, c)
+    total = pick(c)
     for cp in kc:
         cp.wait_recv()
     for i in range(n):
@@ -388,64 +423,113 @@
         cp.start()
         wc.append(cp)
 
-    tile = 512
-
-    def own_rows(t, carry):
-        at = pl.ds(pl.multiple_of(t * tile, tile), tile)
-        basis[at, :] = dot_t(hold[n, at, :], wown[...])
-        return carry
-
-    lax.fori_loop(0, leaf // tile, own_rows, 0)
-
-    back = [OFFSETS.index(((2 - dz) % 2, (4 - dx) % 4)) for dz, dx in OFFSETS]
-    bc = []
-    for i in range(n):
-        wc[back[i]].wait_recv()
-        cp = copy(bout.at[i], bin_.at[i], b_s.at[i], b_r.at[i], peers[i])
-
-        def rows(t, carry, i=i):
-            at = pl.ds(pl.multiple_of(t * tile, tile), tile)
-            bout[i, at, :] = dot_t(hold[i, at, :], win[back[i]]).astype(BF16)
+    def times(j, first, last, weight, put):
+        def rows(t, carry):
+            at = pl.multiple_of(t * tile, tile)
+            put(pl.ds(at, tile), dot_t(partial[j, pl.ds(first + at, tile), :], weight[...]))
             return carry
 
-        lax.fori_loop(0, leaf // tile, rows, 0)
-        cp.start()
-        bc.append(cp)
+        lax.fori_loop(0, (last - first) // tile, rows, 0)
+
+    def store(ref):
+        def put(at, value):
+            ref[at, :] = value.astype(ref.dtype)
+
+        return put
+
+    times(c, 0, leaf, wown, store(basis))
+
+    piece = {o: OFFSETS.index(((2 - o[0]) % 2, (4 - o[1]) % 4)) for o in OFFSETS}
+    at_x = [lax.rem(x + d, 4) for d in range(4)]
+    zpeer = (1 - zh) * 4 + x
+    zc, xc = {}, {}
+    for d in (2, 1, 3, 0):
+        wc[piece[(1, d)]].wait_recv()
+        weight = win.at[piece[(1, d)]]
+        j = (1 - zh) * 4 + at_x[d]
+        times(j, 0, cut, weight, store(zout.at[d]))
+        zc[d] = copy(zout.at[d], zin.at[d], z_s.at[d], z_r.at[d], zpeer)
+        zc[d].start()
+        if d == 0:
+            continue
+        times(j, cut, leaf, weight, store(xout.at[d - 1, 1]))
+        xc[d, 1] = copy(xout.at[d - 1, 1], xin.at[d - 1, 1], x_s.at[d - 1, 1], x_r.at[d - 1, 1], zh * 4 + at_x[d])
+        xc[d, 1].start()
+        wc[piece[(0, d)]].wait_recv()
+        times(zh * 4 + at_x[d], cut, leaf, win.at[piece[(0, d)]], store(xout.at[d - 1, 0]))
+        xc[d, 0] = copy(xout.at[d - 1, 0], xin.at[d - 1, 0], x_s.at[d - 1, 0], x_r.at[d - 1, 0], zh * 4 + at_x[d])
+        xc[d, 0].start()
 
     to_sibling.wait()
     odd = lax.rem(c, 2)
     other = sibling[...]
-    low = jnp.where(odd == 0, skel, other)
-    high = jnp.where(odd == 0, other, skel)
-    both = jnp.concatenate([low, high], axis=0)
+    both = jnp.concatenate([jnp.where(odd == 0, skel, other), jnp.where(odd == 0, other, skel)], axis=0)
     lanes2 = lax.broadcasted_iota(jnp.int32, (rank, 2 * rank), 1)
-    hot = jnp.where(lanes2 == qperm[...], 1.0, 0.0).astype(BF16)
+    order = parent_perm[pl.ds((lax.axis_index("row") * (n + 1) + c) // 2, 1), :]
+    hot = jnp.where(lanes2 == down(order[:, :rank]), 1.0, 0.0).astype(BF16)
     chosen = jnp.dot(hot, both, preferred_element_type=F32).astype(BF16)
     parent[...] = jnp.dot(
         dot_t(skel, chosen), inverse(dot_t(chosen, chosen)), precision=HI, preferred_element_type=F32
     )
 
-    for i in range(n):
-        bc[i].wait_recv()
-
-    def add(t, carry):
+    yc = {}
+    for d in (2, 1, 3):
+        zc[d].wait_recv()
+
+        def put(at, value, d=d):
+            yout[d - 1, at, :] = (value + zin[d, at, :].astype(F32)).astype(BF16)
+
+        times(zh * 4 + at_x[d], 0, cut, win.at[piece[(0, d)]], put)
+        yc[d] = copy(yout.at[d - 1], yin.at[d - 1], y_s.at[d - 1], y_r.at[d - 1], zh * 4 + at_x[d])
+        yc[d].start()
+        if d == 1:
+            for e in (2, 1, 3):
+                xc[e, 1].wait_recv()
+
+            def put_v(at, value):
+                for e in range(3):
+                    value = value + xin[e, 1, at, :].astype(F32)
+                vout[at, :] = value.astype(BF16)
+
+            times(zpeer, cut, leaf, win.at[piece[(1, 0)]], put_v)
+            vc = copy(vout, vin, v_s, v_r, zpeer)
+            vc.start()
+
+    for e in (2, 1, 3):
+        xc[e, 0].wait_recv()
+    zc[0].wait_recv()
+    vc.wait_recv()
+
+    def add_high(t, carry):
+        at = pl.multiple_of(t * tile, tile)
+        value = basis[pl.ds(cut + at, tile), :] + vin[pl.ds(at, tile), :].astype(F32)
+        for e in range(3):
+            value = value + xin[e, 0, pl.ds(at, tile), :].astype(F32)
+        basis[pl.ds(cut + at, tile), :] = value
+        return carry
+
+    lax.fori_loop(0, (leaf - cut) // tile, add_high, 0)
+    for d in (2, 1, 3):
+        yc[d].wait_recv()
+
+    def add_low(t, carry):
         at = pl.ds(pl.multiple_of(t * tile, tile), tile)
-        value = basis[at, :]
-        for i in range(n):
-            value = value + bin_[i, at, :].astype(F32)
+        value = basis[at, :] + zin[0, at, :].astype(F32)
+        for e in range(3):
+            value = value + yin[e, at, :].astype(F32)
         basis[at, :] = value
         return carry
 
-    lax.fori_loop(0, leaf // tile, add, 0)
-    for cp in kc + wc + bc:
+    lax.fori_loop(0, cut // tile, add_low, 0)
+    for cp in kc + wc + list(zc.values()) + list(xc.values()) + list(yc.values()) + [vc]:
         cp.wait_send()
 
 
-def finish(perms, qperm, partial):
-    count, rank = perms.shape
-    width = partial.shape[1]
-    leaf = partial.shape[0] // count
+def finish(perms, parent_perm, partial):
+    count, _, rank = perms.shape
+    leaf, width = partial.shape[1:]
     n = count - 1
+    cut = leaf * 5 // 8
     dma = pltpu.SemaphoreType.DMA
     return pl.pallas_call(
         finish_kernel,
@@ -454,40 +538,42 @@
             jax.ShapeDtypeStruct((leaf, rank), F32),
             jax.ShapeDtypeStruct((rank, rank), F32),
         ),
-        in_specs=[VMEM, VMEM, HBM],
+        in_specs=[VMEM, VMEM, VMEM],
         out_specs=(VMEM, VMEM),
         scratch_shapes=[
             pltpu.VMEM((rank, width), BF16),
-            pltpu.VMEM((count, leaf, width), BF16),
             pltpu.VMEM((n, rank, width), BF16),
             pltpu.VMEM((n, rank, width), BF16),
             pltpu.VMEM((rank, width), BF16),
             pltpu.VMEM((rank, width), BF16),
             pltpu.VMEM((n, rank, width), BF16),
-            pltpu.VMEM((n, leaf, rank), BF16),
-            pltpu.VMEM((n, leaf, rank), BF16),
-            dma((count,)), dma((n,)), dma((n,)), dma, dma,
-            dma((n,)), dma((n,)), dma((n,)), dma((n,)),
+            pltpu.VMEM((4, cut, rank), BF16),
+            pltpu.VMEM((4, cut, rank), BF16),
+            pltpu.VMEM((3, 2, leaf - cut, rank), BF16),
+            pltpu.VMEM((3, 2, leaf - cut, rank), BF16),
+            pltpu.VMEM((3, cut, rank), BF16),
+            pltpu.VMEM((3, cut, rank), BF16),
+            pltpu.VMEM((leaf - cut, rank), BF16),
+            pltpu.VMEM((leaf - cut, rank), BF16),
+            dma((n,)), dma((n,)), dma, dma, dma((n,)), dma((n,)),
+            dma((4,)), dma((4,)), dma((3, 2)), dma((3, 2)), dma((3,)), dma((3,)), dma, dma,
         ],
         compiler_params=pltpu.CompilerParams(
-            collective_id=1, has_side_effects=True, vmem_limit_bytes=40 << 20
+            collective_id=1, has_side_effects=True, vmem_limit_bytes=24 << 20
         ),
-    )(perms[:, :, None], qperm[:, None], partial)
+    )(perms, parent_perm, partial)
 
 
 def local(blocks, block_row, block_col, random_cols, leaf_perm, parent_perm):
     n_col = lax.axis_size("col")
     leaf_rows, width = random_cols.shape[2:]
     size = blocks.shape[1]
-    nrows = leaf_rows * n_col // size
     rank = parent_perm.shape[1] // 2
-    slots, steps, total = schedule(block_row, block_col, nrows)
-    own_perm = jnp.broadcast_to(leaf_perm[:, :rank], (8, rank))
-    gathered, perms = gather(random_cols.reshape(leaf_rows, width), own_perm)
-    partial_value = spmm(slots, steps, total, blocks, gathered.reshape(-1, size, width), nrows)
-    device = lax.axis_index("row") * n_col + lax.axis_index("col")
-    qperm = lax.dynamic_index_in_dim(parent_perm, device // 2, 0, keepdims=False)[:rank]
-    return finish(perms[:, 0], qperm, partial_value.reshape(nrows * size, width))
+    gathered, perms, plan = gather(
+        random_cols.reshape(leaf_rows, width), block_row, block_col, leaf_perm[0, :rank]
+    )
+    partial_value = spmm(plan, blocks, gathered.reshape(-1, size, width), n_col, leaf_rows)
+    return finish(perms, parent_perm, partial_value)
 
 
 def solution(mesh):

time: 192 us -> 146 us (0.76)
  Pallas kernels: 178 us -> 141 us
  local copies, waits for them, and re-layouts: 8.15 us -> 3.49 us
  other arithmetic: 4.46 us -> 0.71 us
    pallas_call x1, Pallas kernels: 84.1 us -> 60.4 us  [finish(): pl.pallas_call(finish_kernel, name='finish', out_shape=(jax.ShapeDtypeStr...]
    pallas_call x1, Pallas kernels: 26.9 us -> 15.5 us  [spmm(): pl.pallas_call(spmm_kernel, name='spmm', out_shape=jax.ShapeDtypeStruct((...]
    reduce_sum x7 -> x0, other arithmetic: 3.76 us -> none  [the longest x1 0.99 us: schedule(): within = jnp.sum(same.astype(jnp.int32), axis=1)]
    unnamed x6 -> x8, local copies, waits for them, and re-layouts: 5.8 us -> 2.83 us
where the time goes in v3:
time: 146 us
  Pallas kernels  141 us (97%)
  local copies, waits for them, and re-layouts  3.49 us (2%)
    pallas_call x1, Pallas kernels, gather(): pl.pallas_call(gather_kernel, name='gather', out_shape=(jax.ShapeDtypeStr...  65.5 us
    pallas_call x1, Pallas kernels, finish(): pl.pallas_call(finish_kernel, name='finish', out_shape=(jax.ShapeDtypeStr...  60.4 us
    pallas_call x1, Pallas kernels, spmm(): pl.pallas_call(spmm_kernel, name='spmm', out_shape=jax.ShapeDtypeStruct((...  15.5 us

profile of v3, /device:TPU:0, one launch (start us, length us, event | category | flops | bytes accessed | tf_op | source)
XLA Modules:
  0.0 146.3 jit_solution(8492953671317983498)
XLA Ops:
  0.6 0.7 slice_bitcast_fusion
  1.3 0.7 pad_add_fusion
  2.0 0.0 copy-start.2
  2.0 1.2 copy-done.2
  3.2 0.0 copy-start
  3.2 65.5 %gather.1 = (bf16[32768,256]{1,0:T(8,128)(2,1)S(1)}, s32[8,8,128]{2,1,0:T(8,128)S(1)}, s32[8,128]{1,0:T(8,128)S(1)}) custom-call(bf16[2048,256]{1,0:T(8,128)(2,1)S(1)} %bitcast.5, s32[1,896]{1,0:T(1,128)S(1)} %broadcast_in_dim.3.ints), custom_call_target="tpu_custom_call" | custom-call | flops 60000002048 | bytes 40000000 | tf_op jit(solution)/shard_map/gather/pallas_call | solution.py:232
  68.7 0.0 copy-done
  68.7 0.0 copy-start.1
  68.8 15.5 %spmm.1.partial = bf16[8,2048,256]{2,1,0:T(8,128)(2,1)S(1)} custom-call(s32[8,128]{1,0:T(8,128)S(1)} %get-tuple-element.6.plan, bf16[384,128,128]{2,1,0:T(8,128)(2,1)S(1)} %copy-done, bf16[256,128,256]{2,1,0:T(8,128)(2,1)S(1)} %bitcast.4), custom_call_target="tpu_custom_call" | custom-call | tf_op jit(solution)/shard_map/spmm/pallas_call | solution.py:295
  84.3 0.0 copy-done.1
  84.3 60.4 %finish.1 = (f32[2048,128]{1,0:T(8,128)S(1)}, f32[128,128]{1,0:T(8,128)S(1)}) custom-call(s32[8,8,128]{2,1,0:T(8,128)S(1)} %get-tuple-element.5.perms, s32[64,256]{1,0:T(8,128)S(1)} %copy-done.1, bf16[8,2048,256]{2,1,0:T(8,128)(2,1)S(1)} %spmm.1.partial), custom_call_target="tpu_custom_call" | custom-call | tf_op jit(solution)/shard_map/finish/pallas_call | solution.py:534
  144.7 1.0 copy.10
  145.7 0.6 copy.11
  (1 shorter events, 0.0 us)
Async XLA Ops:
  2.0 1.2 copy-start.2
  3.2 65.5 %copy-start = (bf16[384,128,128]{2,1,0:T(8,128)(2,1)S(1)}, bf16[384,128,128]{2,1,0:T(8,128)(2,1)}, u32[]{:S(2)}) copy-start(bf16[384,128,128]{2,1,0:T(8,128)(2,1)} %blocks.1) | copy-start | bytes 37748740
  68.7 15.5 %copy-start.1 = (s32[64,256]{1,0:T(8,128)S(1)}, s32[64,256]{1,0:T(8,128)}, u32[]{:S(2)}) copy-start(s32[64,256]{1,0:T(8,128)} %parent_perm.1) | copy-start | bytes 196612

commit v4 on v3

--- a/solution.py
+++ b/solution.py
@@ -250,7 +250,7 @@
     )(own, ints)
 
 
-UNROLL = 4
+UNROLL = 8
 
 
 def spmm_kernel(plan, blocks, rand, out, acc):

time: 146 us -> 141 us (0.966)
  Pallas kernels: 141 us -> 136 us
    pallas_call x1, Pallas kernels: 15.5 us -> 10.6 us  [spmm(): pl.pallas_call(spmm_kernel, name='spmm', out_shape=jax.ShapeDtypeStruct((...]
where the time goes in v4:
time: 141 us
  Pallas kernels  136 us (96%)
  local copies, waits for them, and re-layouts  3.49 us (2%)
    pallas_call x1, Pallas kernels, gather(): pl.pallas_call(gather_kernel, name='gather', out_shape=(jax.ShapeDtypeStr...  65.5 us
    pallas_call x1, Pallas kernels, finish(): pl.pallas_call(finish_kernel, name='finish', out_shape=(jax.ShapeDtypeStr...  60.2 us
    pallas_call x1, Pallas kernels, spmm(): pl.pallas_call(spmm_kernel, name='spmm', out_shape=jax.ShapeDtypeStruct((...  10.6 us
    unnamed x8, local copies, waits for them, and re-layouts  2.83 us

profile of v4, /device:TPU:0, one launch (start us, length us, event | category | flops | bytes accessed | tf_op | source)
XLA Modules:
  0.0 141.1 jit_solution(3524165821212718421)
XLA Ops:
  0.6 0.7 slice_bitcast_fusion
  1.3 0.7 pad_add_fusion
  2.0 0.0 copy-start.2
  2.0 1.2 copy-done.2
  3.2 0.0 copy-start
  3.2 65.5 %gather.1 = (bf16[32768,256]{1,0:T(8,128)(2,1)S(1)}, s32[8,8,128]{2,1,0:T(8,128)S(1)}, s32[8,128]{1,0:T(8,128)S(1)}) custom-call(bf16[2048,256]{1,0:T(8,128)(2,1)S(1)} %bitcast.5, s32[1,896]{1,0:T(1,128)S(1)} %broadcast_in_dim.3.ints), custom_call_target="tpu_custom_call" | custom-call | flops 60000002048 | bytes 40000000 | tf_op jit(solution)/shard_map/gather/pallas_call | solution.py:232
  68.7 0.0 copy-done
  68.7 0.0 copy-start.1
  68.8 10.6 %spmm.1.partial = bf16[8,2048,256]{2,1,0:T(8,128)(2,1)S(1)} custom-call(s32[8,128]{1,0:T(8,128)S(1)} %get-tuple-element.6.plan, bf16[384,128,128]{2,1,0:T(8,128)(2,1)S(1)} %copy-done, bf16[256,128,256]{2,1,0:T(8,128)(2,1)S(1)} %bitcast.4), custom_call_target="tpu_custom_call" | custom-call | tf_op jit(solution)/shard_map/spmm/pallas_call | solution.py:295
  79.4 0.0 copy-done.1
  79.4 60.2 %finish.1 = (f32[2048,128]{1,0:T(8,128)S(1)}, f32[128,128]{1,0:T(8,128)S(1)}) custom-call(s32[8,8,128]{2,1,0:T(8,128)S(1)} %get-tuple-element.5.perms, s32[64,256]{1,0:T(8,128)S(1)} %copy-done.1, bf16[8,2048,256]{2,1,0:T(8,128)(2,1)S(1)} %spmm.1.partial), custom_call_target="tpu_custom_call" | custom-call | tf_op jit(solution)/shard_map/finish/pallas_call | solution.py:534
  139.5 1.0 copy.10
  140.5 0.6 copy.11
  (1 shorter events, 0.0 us)
Async XLA Ops:
  2.0 1.2 copy-start.2
  3.2 65.5 %copy-start = (bf16[384,128,128]{2,1,0:T(8,128)(2,1)S(1)}, bf16[384,128,128]{2,1,0:T(8,128)(2,1)}, u32[]{:S(2)}) copy-start(bf16[384,128,128]{2,1,0:T(8,128)(2,1)} %blocks.1) | copy-start | bytes 37748740
  68.7 10.6 %copy-start.1 = (s32[64,256]{1,0:T(8,128)S(1)}, s32[64,256]{1,0:T(8,128)}, u32[]{:S(2)}) copy-start(s32[64,256]{1,0:T(8,128)} %parent_perm.1) | copy-start | bytes 196612

commit v5 on v4

--- a/solution.py
+++ b/solution.py
@@ -95,8 +95,8 @@
         pl.semaphore_signal(barrier, inc=1, device_id={"col": j}, device_id_type=MESH)
     keep = pltpu.make_async_copy(own, out.at[pl.ds(pl.multiple_of(r * size, size), size)], local_sem)
     keep.start()
-    n_blocks = (ints.shape[1] - perm.shape[1]) // 2
-    perm[...] = jnp.broadcast_to(ints[:, 2 * n_blocks :], perm.shape)
+    n_blocks = (ints.shape[1] - size) // 2
+    perm[...] = jnp.broadcast_to(ints[:, 2 * n_blocks : 2 * n_blocks + perm.shape[1]], perm.shape)
     keep_perm = pltpu.make_async_copy(perm, perms.at[lax.axis_index("col")], perm_local)
     keep_perm.start()
     pl.semaphore_wait(barrier, 4 + len(peers))
@@ -223,10 +223,9 @@
         cp.wait()
 
 
-def gather(own, rows, cols, order):
+def gather(own, rows, cols, order, rank):
     size, width = own.shape
     count, n_col = lax.axis_size("row"), lax.axis_size("col")
-    rank = order.shape[0]
     ints = jnp.concatenate([rows, cols, order])[None, :]
     dma = pltpu.SemaphoreType.DMA
     return pl.pallas_call(
@@ -365,8 +364,8 @@
 
 def finish_kernel(
     perms, parent_perm, partial, basis, parent,
-    mine, ksend, kin, sibling, wown, win, zout, zin, xout, xin, yout, yin, vout, vin,
-    k_s, k_r, s_s, s_r, w_s, w_r, z_s, z_r, x_s, x_r, y_s, y_r, v_s, v_r,
+    mine, ksend, kin, sibling, wown, win, zout, zin, xout, xin, yout, yin, vout, vin, rzin, rxin,
+    k_s, k_r, s_s, s_r, w_s, w_r, z_s, z_r, x_s, x_r, y_s, y_r, v_s, v_r, rz_s, rz_r, rx_s, rx_r,
 ):
     c = lax.axis_index("col")
     zh, x = c // 4, lax.rem(c, 4)
@@ -374,8 +373,9 @@
     peers = col_peers()
     n = len(peers)
     rank, width = mine.shape
-    cut = zout.shape[1]
-    tile = 256
+    cut, raw = zout.shape[1], rzin.shape[1]
+    top, last = leaf - 2 * raw, leaf - raw
+    tile = 128
 
     barrier = pltpu.get_barrier_semaphore()
     for j in peers:
@@ -412,6 +412,22 @@
     mine[...] = total.astype(BF16)
     to_sibling = copy(mine, sibling, s_s, s_r, c + 1 - 2 * lax.rem(c, 2))
     to_sibling.start()
+    at_x = [lax.rem(x + d, 4) for d in range(4)]
+    zpeer = (1 - zh) * 4 + x
+    rz, rx = {}, {}
+    for d in (2, 1, 3, 0):
+        rz[d] = copy(
+            partial.at[(1 - zh) * 4 + at_x[d], pl.ds(top, raw)], rzin.at[d], rz_s.at[d], rz_r.at[d], zpeer
+        )
+        rz[d].start()
+        if d == 0:
+            continue
+        for h in range(2):
+            rx[d, h] = copy(
+                partial.at[lax.rem(zh + h, 2) * 4 + at_x[d], pl.ds(last, raw)],
+                rxin.at[d - 1, h], rx_s.at[d - 1, h], rx_r.at[d - 1, h], zh * 4 + at_x[d],
+            )
+            rx[d, h].start()
 
     skel = mine[...]
     wown[...] = jnp.dot(
@@ -424,12 +440,8 @@
         wc.append(cp)
 
     def times(j, first, last, weight, put):
-        def rows(t, carry):
-            at = pl.multiple_of(t * tile, tile)
-            put(pl.ds(at, tile), dot_t(partial[j, pl.ds(first + at, tile), :], weight[...]))
-            return carry
-
-        lax.fori_loop(0, (last - first) // tile, rows, 0)
+        value = dot_t(partial[j, pl.ds(first, last - first), :], weight[...])
+        put(pl.ds(0, last - first), value)
 
     def store(ref):
         def put(at, value):
@@ -437,11 +449,9 @@
 
         return put
 
-    times(c, 0, leaf, wown, store(basis))
+    times(c, 0, top, wown, store(basis))
 
     piece = {o: OFFSETS.index(((2 - o[0]) % 2, (4 - o[1]) % 4)) for o in OFFSETS}
-    at_x = [lax.rem(x + d, 4) for d in range(4)]
-    zpeer = (1 - zh) * 4 + x
     zc, xc = {}, {}
     for d in (2, 1, 3, 0):
         wc[piece[(1, d)]].wait_recv()
@@ -452,11 +462,11 @@
         zc[d].start()
         if d == 0:
             continue
-        times(j, cut, leaf, weight, store(xout.at[d - 1, 1]))
+        times(j, cut, top, weight, store(xout.at[d - 1, 1]))
         xc[d, 1] = copy(xout.at[d - 1, 1], xin.at[d - 1, 1], x_s.at[d - 1, 1], x_r.at[d - 1, 1], zh * 4 + at_x[d])
         xc[d, 1].start()
         wc[piece[(0, d)]].wait_recv()
-        times(zh * 4 + at_x[d], cut, leaf, win.at[piece[(0, d)]], store(xout.at[d - 1, 0]))
+        times(zh * 4 + at_x[d], cut, top, win.at[piece[(0, d)]], store(xout.at[d - 1, 0]))
         xc[d, 0] = copy(xout.at[d - 1, 0], xin.at[d - 1, 0], x_s.at[d - 1, 0], x_r.at[d - 1, 0], zh * 4 + at_x[d])
         xc[d, 0].start()
 
@@ -472,6 +482,18 @@
         dot_t(skel, chosen), inverse(dot_t(chosen, chosen)), precision=HI, preferred_element_type=F32
     )
 
+    def over_z(d):
+        rz[d].wait_recv()
+        return (partial[zh * 4 + at_x[d], pl.ds(top, raw), :].astype(F32) + rzin[d].astype(F32)).astype(BF16)
+
+    def over_x(h):
+        for e in (2, 1, 3):
+            rx[e, h].wait_recv()
+        value = partial[lax.rem(zh + h, 2) * 4 + x, pl.ds(last, raw), :].astype(F32)
+        for e in range(3):
+            value = value + rxin[e, h].astype(F32)
+        return value.astype(BF16)
+
     yc = {}
     for d in (2, 1, 3):
         zc[d].wait_recv()
@@ -480,6 +502,7 @@
             yout[d - 1, at, :] = (value + zin[d, at, :].astype(F32)).astype(BF16)
 
         times(zh * 4 + at_x[d], 0, cut, win.at[piece[(0, d)]], put)
+        yout[d - 1, pl.ds(cut, raw), :] = dot_t(over_z(d), win[piece[(0, d)]]).astype(BF16)
         yc[d] = copy(yout.at[d - 1], yin.at[d - 1], y_s.at[d - 1], y_r.at[d - 1], zh * 4 + at_x[d])
         yc[d].start()
         if d == 1:
@@ -491,10 +514,13 @@
                     value = value + xin[e, 1, at, :].astype(F32)
                 vout[at, :] = value.astype(BF16)
 
-            times(zpeer, cut, leaf, win.at[piece[(1, 0)]], put_v)
+            times(zpeer, cut, top, win.at[piece[(1, 0)]], put_v)
+            vout[pl.ds(top - cut, raw), :] = dot_t(over_x(1), win[piece[(1, 0)]]).astype(BF16)
             vc = copy(vout, vin, v_s, v_r, zpeer)
             vc.start()
 
+    basis[pl.ds(top, raw), :] = dot_t(over_z(0), wown[...])
+    basis[pl.ds(last, raw), :] = dot_t(over_x(0), wown[...])
     for e in (2, 1, 3):
         xc[e, 0].wait_recv()
     zc[0].wait_recv()
@@ -508,7 +534,8 @@
         basis[pl.ds(cut + at, tile), :] = value
         return carry
 
-    lax.fori_loop(0, (leaf - cut) // tile, add_high, 0)
+    lax.fori_loop(0, (top - cut) // tile, add_high, 0)
+    basis[pl.ds(last, raw), :] = basis[pl.ds(last, raw), :] + vin[pl.ds(top - cut, raw), :].astype(F32)
     for d in (2, 1, 3):
         yc[d].wait_recv()
 
@@ -521,7 +548,11 @@
         return carry
 
     lax.fori_loop(0, cut // tile, add_low, 0)
-    for cp in kc + wc + list(zc.values()) + list(xc.values()) + list(yc.values()) + [vc]:
+    value = basis[pl.ds(top, raw), :]
+    for e in range(3):
+        value = value + yin[e, pl.ds(cut, raw), :].astype(F32)
+    basis[pl.ds(top, raw), :] = value
+    for cp in kc + wc + list(zc.values()) + list(xc.values()) + list(yc.values()) + list(rz.values()) + list(rx.values()) + [vc]:
         cp.wait_send()
 
 
@@ -529,7 +560,8 @@
     count, _, rank = perms.shape
     leaf, width = partial.shape[1:]
     n = count - 1
-    cut = leaf * 5 // 8
+    raw = leaf // 16
+    cut = leaf * 9 // 16
     dma = pltpu.SemaphoreType.DMA
     return pl.pallas_call(
         finish_kernel,
@@ -549,14 +581,17 @@
             pltpu.VMEM((n, rank, width), BF16),
             pltpu.VMEM((4, cut, rank), BF16),
             pltpu.VMEM((4, cut, rank), BF16),
-            pltpu.VMEM((3, 2, leaf - cut, rank), BF16),
-            pltpu.VMEM((3, 2, leaf - cut, rank), BF16),
-            pltpu.VMEM((3, cut, rank), BF16),
-            pltpu.VMEM((3, cut, rank), BF16),
-            pltpu.VMEM((leaf - cut, rank), BF16),
-            pltpu.VMEM((leaf - cut, rank), BF16),
+            pltpu.VMEM((3, 2, leaf - cut - 2 * raw, rank), BF16),
+            pltpu.VMEM((3, 2, leaf - cut - 2 * raw, rank), BF16),
+            pltpu.VMEM((3, cut + raw, rank), BF16),
+            pltpu.VMEM((3, cut + raw, rank), BF16),
+            pltpu.VMEM((leaf - cut - raw, rank), BF16),
+            pltpu.VMEM((leaf - cut - raw, rank), BF16),
+            pltpu.VMEM((4, raw, width), BF16),
+            pltpu.VMEM((3, 2, raw, width), BF16),
             dma((n,)), dma((n,)), dma, dma, dma((n,)), dma((n,)),
             dma((4,)), dma((4,)), dma((3, 2)), dma((3, 2)), dma((3,)), dma((3,)), dma, dma,
+            dma((4,)), dma((4,)), dma((3, 2)), dma((3, 2)),
         ],
         compiler_params=pltpu.CompilerParams(
             collective_id=1, has_side_effects=True, vmem_limit_bytes=24 << 20
@@ -570,7 +605,7 @@
     size = blocks.shape[1]
     rank = parent_perm.shape[1] // 2
     gathered, perms, plan = gather(
-        random_cols.reshape(leaf_rows, width), block_row, block_col, leaf_perm[0, :rank]
+        random_cols.reshape(leaf_rows, width), block_row, block_col, leaf_perm.reshape(-1), rank
     )
     partial_value = spmm(plan, blocks, gathered.reshape(-1, size, width), n_col, leaf_rows)
     return finish(perms, parent_perm, partial_value)

time: 141 us -> 139 us (0.986)
  Pallas kernels: 136 us -> 134 us
    pallas_call x1, Pallas kernels: 60.2 us -> 58.3 us  [finish(): pl.pallas_call(finish_kernel, name='finish', out_shape=(jax.ShapeDtypeStr...]
where the time goes in v5:
time: 139 us; the launch traced here: 138 us
  Pallas kernels  134 us (96%)
  local copies, waits for them, and re-layouts  2.84 us (2%)
    pallas_call x1, Pallas kernels, gather(): pl.pallas_call(gather_kernel, name='gather', out_shape=(jax.ShapeDtypeStr...  65.5 us
    pallas_call x1, Pallas kernels, finish(): pl.pallas_call(finish_kernel, name='finish', out_shape=(jax.ShapeDtypeStr...  58.3 us
    pallas_call x1, Pallas kernels, spmm(): pl.pallas_call(spmm_kernel, name='spmm', out_shape=jax.ShapeDtypeStruct((...  10.3 us
    unnamed x8, local copies, waits for them, and re-layouts  2.83 us

profile of v5, /device:TPU:0, one launch (start us, length us, event | category | flops | bytes accessed | tf_op | source)
XLA Modules:
  0.0 138.3 jit_solution(3814471688395510495)
XLA Ops:
  0.6 0.7 pad_add_fusion
  1.4 0.0 copy-start.2
  1.4 1.2 copy-done.2
  2.6 0.0 copy-start
  2.6 65.5 %gather.1 = (bf16[32768,256]{1,0:T(8,128)(2,1)S(1)}, s32[8,8,128]{2,1,0:T(8,128)S(1)}, s32[8,128]{1,0:T(8,128)S(1)}) custom-call(bf16[2048,256]{1,0:T(8,128)(2,1)S(1)} %bitcast.4, s32[1,2816]{1,0:T(1,128)S(1)} %broadcast_in_dim.3.ints), custom_call_target="tpu_custom_call" | custom-call | flops 60000002048 | bytes 40000000 | tf_op jit(solution)/shard_map/gather/pallas_call | solution.py:231
  68.1 0.0 copy-done
  68.1 0.0 copy-start.1
  68.1 10.3 %spmm.1.partial = bf16[8,2048,256]{2,1,0:T(8,128)(2,1)S(1)} custom-call(s32[8,128]{1,0:T(8,128)S(1)} %get-tuple-element.6.plan, bf16[384,128,128]{2,1,0:T(8,128)(2,1)S(1)} %copy-done, bf16[256,128,256]{2,1,0:T(8,128)(2,1)S(1)} %bitcast.3), custom_call_target="tpu_custom_call" | custom-call | tf_op jit(solution)/shard_map/spmm/pallas_call | solution.py:294
  78.4 0.0 copy-done.1
  78.4 58.3 %finish.1 = (f32[2048,128]{1,0:T(8,128)S(1)}, f32[128,128]{1,0:T(8,128)S(1)}) custom-call(s32[8,8,128]{2,1,0:T(8,128)S(1)} %get-tuple-element.5.perms, s32[64,256]{1,0:T(8,128)S(1)} %copy-done.1, bf16[8,2048,256]{2,1,0:T(8,128)(2,1)S(1)} %spmm.1.partial), custom_call_target="tpu_custom_call" | custom-call | tf_op jit(solution)/shard_map/finish/pallas_call | solution.py:566
  136.7 1.0 copy.10
  137.7 0.6 copy.11
  (1 shorter events, 0.0 us)
Async XLA Ops:
  1.4 1.2 copy-start.2
  2.6 65.5 %copy-start = (bf16[384,128,128]{2,1,0:T(8,128)(2,1)S(1)}, bf16[384,128,128]{2,1,0:T(8,128)(2,1)}, u32[]{:S(2)}) copy-start(bf16[384,128,128]{2,1,0:T(8,128)(2,1)} %blocks.1) | copy-start | bytes 37748740
  68.1 10.3 %copy-start.1 = (s32[64,256]{1,0:T(8,128)S(1)}, s32[64,256]{1,0:T(8,128)}, u32[]{:S(2)}) copy-start(s32[64,256]{1,0:T(8,128)} %parent_perm.1) | copy-start | bytes 196612

commit v6 on v5

--- a/solution.py
+++ b/solution.py
@@ -599,6 +599,30 @@
     )(perms, parent_perm, partial)
 
 
+def deliver_kernel(basis, parent, basis_out, parent_out, sems):
+    first = pltpu.make_async_copy(basis, basis_out, sems.at[0])
+    second = pltpu.make_async_copy(parent, parent_out, sems.at[1])
+    first.start()
+    second.start()
+    first.wait()
+    second.wait()
+
+
+def deliver(basis, parent):
+    return pl.pallas_call(
+        deliver_kernel,
+        name="deliver",
+        out_shape=(
+            jax.ShapeDtypeStruct(basis.shape, basis.dtype),
+            jax.ShapeDtypeStruct(parent.shape, parent.dtype),
+        ),
+        in_specs=[VMEM, VMEM],
+        out_specs=(HBM, HBM),
+        scratch_shapes=[pltpu.SemaphoreType.DMA((2,))],
+        compiler_params=pltpu.CompilerParams(vmem_limit_bytes=4 << 20),
+    )(basis, parent)
+
+
 def local(blocks, block_row, block_col, random_cols, leaf_perm, parent_perm):
     n_col = lax.axis_size("col")
     leaf_rows, width = random_cols.shape[2:]
@@ -608,7 +632,7 @@
         random_cols.reshape(leaf_rows, width), block_row, block_col, leaf_perm.reshape(-1), rank
     )
     partial_value = spmm(plan, blocks, gathered.reshape(-1, size, width), n_col, leaf_rows)
-    return finish(perms, parent_perm, partial_value)
+    return deliver(*finish(perms, parent_perm, partial_value))
 
 
 def solution(mesh):

time: 139 us -> 138 us (level)
  local copies, waits for them, and re-layouts: 2.84 us -> 1.24 us
    unnamed x8 -> x6, local copies, waits for them, and re-layouts: 2.83 us -> 1.23 us
where the time goes in v6:
time: 138 us
  Pallas kernels  135 us (98%)
    pallas_call x1, Pallas kernels, gather(): pl.pallas_call(gather_kernel, name='gather', out_shape=(jax.ShapeDtypeStr...  65.5 us
    pallas_call x1, Pallas kernels, finish(): pl.pallas_call(finish_kernel, name='finish', out_shape=(jax.ShapeDtypeStr...  58.3 us
    pallas_call x1, Pallas kernels, spmm(): pl.pallas_call(spmm_kernel, name='spmm', out_shape=jax.ShapeDtypeStruct((...  10.6 us

profile of v6, /device:TPU:0, one launch (start us, length us, event | category | flops | bytes accessed | tf_op | source)
XLA Modules:
  0.0 138.1 jit_solution(13151743798738527109)
XLA Ops:
  0.6 0.7 pad_add_fusion
  1.4 0.0 copy-start.2
  1.4 1.2 copy-done.2
  2.6 0.0 copy-start
  2.6 65.5 %gather.1 = (bf16[32768,256]{1,0:T(8,128)(2,1)S(1)}, s32[8,8,128]{2,1,0:T(8,128)S(1)}, s32[8,128]{1,0:T(8,128)S(1)}) custom-call(bf16[2048,256]{1,0:T(8,128)(2,1)S(1)} %bitcast.4, s32[1,2816]{1,0:T(1,128)S(1)} %broadcast_in_dim.3.ints), custom_call_target="tpu_custom_call" | custom-call | flops 60000002048 | bytes 40000000 | tf_op jit(solution)/shard_map/gather/pallas_call | solution.py:231
  68.1 0.0 copy-done
  68.1 0.0 copy-start.1
  68.1 10.6 %spmm.1.partial = bf16[8,2048,256]{2,1,0:T(8,128)(2,1)S(1)} custom-call(s32[8,128]{1,0:T(8,128)S(1)} %get-tuple-element.8.plan, bf16[384,128,128]{2,1,0:T(8,128)(2,1)S(1)} %copy-done, bf16[256,128,256]{2,1,0:T(8,128)(2,1)S(1)} %bitcast.3), custom_call_target="tpu_custom_call" | custom-call | tf_op jit(solution)/shard_map/spmm/pallas_call | solution.py:294
  78.8 0.0 copy-done.1
  78.8 58.3 %finish.1 = (f32[2048,128]{1,0:T(8,128)S(1)}, f32[128,128]{1,0:T(8,128)S(1)}) custom-call(s32[8,8,128]{2,1,0:T(8,128)S(1)} %get-tuple-element.7.perms, s32[64,256]{1,0:T(8,128)S(1)} %copy-done.1, bf16[8,2048,256]{2,1,0:T(8,128)(2,1)S(1)} %spmm.1.partial), custom_call_target="tpu_custom_call" | custom-call | tf_op jit(solution)/shard_map/finish/pallas_call | solution.py:566
  137.1 1.0 deliver.1
  (1 shorter events, 0.0 us)
Async XLA Ops:
  1.4 1.2 copy-start.2
  2.6 65.5 %copy-start = (bf16[384,128,128]{2,1,0:T(8,128)(2,1)S(1)}, bf16[384,128,128]{2,1,0:T(8,128)(2,1)}, u32[]{:S(2)}) copy-start(bf16[384,128,128]{2,1,0:T(8,128)(2,1)} %blocks.1) | copy-start | bytes 37748740
  68.1 10.6 %copy-start.1 = (s32[64,256]{1,0:T(8,128)S(1)}, s32[64,256]{1,0:T(8,128)}, u32[]{:S(2)}) copy-start(s32[64,256]{1,0:T(8,128)} %parent_perm.1) | copy-start | bytes 196612
